TPU v7x, 512 devices: a whole 4x4x16 slice. The times are simulated.
512 devices in a mesh: grp: 16 (over z_hi, y), seq: 32 (over x, z_lo, core).
Axes of the slice: x: 4, y: 4, z: 16 (z_hi: 4, z_lo: 4; z = z_hi * 4 + z_lo), core: 2. Of those that a mesh axis runs over, the one named last changes fastest.
Arguments:
- tokens: bfloat16 [65536, 768], P(('grp', 'seq')), may hold values from -40 to 40
- tile_pos: int32 [2, 65536], P(None, ('grp', 'seq')), may hold values from 0 to 1023
- w_qkv: bfloat16 [768, 2304], replicated, may hold values from -1 to 1
- w_out: bfloat16 [768, 768], P('grp'), may hold values from -0.21875 to 0.21875
Outputs:
- output: bfloat16 [65536, 768], P(('grp', 'seq'))
All inputs are finite; a program needn't handle non-finite values.
Results may differ from a plain program's by a relative error of at most 0.011.
Values may be sent and summed in bfloat16 or wider, within the bound.
A program may use at most 64 MiB of HBM per device.

v0:
```python
import jax
import jax.numpy as jnp
import numpy as np
from jax import lax
from jax.sharding import PartitionSpec as P

H = 16


def swapped(value, axis, bit):
    mask = 2**bit
    pairs = [(source, source ^ mask) for source in range(lax.axis_size(axis))]
    return lax.ppermute(value, axis, pairs)


def embed(tile_pos, feat_width):
    quarter = feat_width // 4
    omega = 10000.0 ** (-jnp.arange(quarter, dtype=jnp.float32) / quarter)
    across = tile_pos[0].astype(jnp.float32)[:, None] * omega[None, :]
    downward = tile_pos[1].astype(jnp.float32)[:, None] * omega[None, :]
    return jnp.concatenate(
        [jnp.sin(across), jnp.cos(across), jnp.sin(downward), jnp.cos(downward)], axis=1
    )


def attend(queries, keys_all, values_all):
    score_scale = queries.shape[2] ** (-0.5)
    scores = (
        jnp.einsum("qhd,khd->hqk", queries, keys_all, preferred_element_type=jnp.float32)
        * score_scale
    )
    top = jnp.max(scores, axis=2)
    weights = jnp.exp(scores - top[:, :, None])
    total = jnp.sum(weights, axis=2)
    mixed = jnp.einsum(
        "hqk,khd->qhd", weights.astype(jnp.bfloat16), values_all, preferred_element_type=jnp.float32
    )
    return (top.T, total.T, mixed)


def select_rows(array, dilation, head_count):
    lead = array.shape[:-2]
    row_count = array.shape[-2]
    feat_width = array.shape[-1]
    head_dim = feat_width // head_count
    head_ids = np.arange(head_count)
    offsets = head_ids % dilation
    shaped = array.reshape(lead + (row_count // dilation, dilation, head_count, head_dim))
    chosen = shaped[..., offsets, head_ids, :]
    return chosen.reshape(lead + (row_count // dilation, feat_width))


def repeat_rows(block, dilation, row_count):
    shaped = jnp.broadcast_to(block[:, None], (block.shape[0], dilation) + block.shape[1:])
    return shaped.reshape((row_count,) + block.shape[1:])


def pair_up(mine, partner, upper):
    lower = jnp.where(upper, partner, mine)
    higher = jnp.where(upper, mine, partner)
    return jnp.concatenate([lower, higher], axis=1)


def shards(tokens, tile_pos, w_qkv, w_out):
    row_count, feat_width = tokens.shape
    head_count = H
    head_dim = feat_width // head_count
    embedded = (tokens.astype(jnp.float32) + embed(tile_pos, feat_width)).astype(jnp.bfloat16)
    qkv = jnp.dot(embedded, w_qkv, preferred_element_type=jnp.float32).astype(jnp.bfloat16)
    query_rows = qkv[:, :feat_width]
    queries = query_rows.reshape(row_count, head_count, head_dim)
    stacked = jnp.stack([qkv[:, feat_width : 2 * feat_width], qkv[:, 2 * feat_width :]])
    mid_rate = lax.axis_size("seq") // 4
    third_rate = lax.axis_size("seq")
    far_rate = lax.axis_size("grp") * lax.axis_size("seq") // 4
    seq_place = lax.axis_index("seq")
    grp_place = lax.axis_index("grp")
    near_kv = stacked
    for bit_index in range(2):
        partner = swapped(near_kv, "seq", bit_index)
        near_kv = pair_up(near_kv, partner, seq_place // 2**bit_index % 2 == 1)
    mid_kv = select_rows(stacked, mid_rate, head_count)
    third_kv = select_rows(stacked, third_rate, head_count)
    far_kv = select_rows(stacked, far_rate, head_count)
    mid_all, third_all = (
        lax.all_gather(mid_kv, "seq", axis=1, tiled=True),
        lax.all_gather(third_kv, "seq", axis=1, tiled=True),
    )
    far_all = lax.all_gather(far_kv, ("grp", "seq"), axis=1, tiled=True)
    for bit_index in range(2):
        partner = swapped(third_all, "grp", bit_index)
        third_all = pair_up(third_all, partner, grp_place // 2**bit_index % 2 == 1)
    near_keys = near_kv[0].reshape(-1, head_count, head_dim)
    near_values = near_kv[1].reshape(-1, head_count, head_dim)
    head_block = min(4, head_count)
    near_parts = [
        attend(
            queries[:, first_head : first_head + head_block],
            near_keys[:, first_head : first_head + head_block],
            near_values[:, first_head : first_head + head_block],
        )
        for first_head in range(0, head_count, head_block)
    ]
    near_member = jnp.asarray(np.ones((row_count, head_count), dtype=bool))
    results = [
        (
            jnp.concatenate([item[0] for item in near_parts], axis=1),
            jnp.concatenate([item[1] for item in near_parts], axis=1),
            jnp.concatenate([item[2] for item in near_parts], axis=1),
            near_member,
        )
    ]
    head_ids = np.arange(head_count)
    row_ids = np.arange(row_count)
    for gathered, dilation in ((mid_all, mid_rate), (third_all, third_rate), (far_all, far_rate)):
        chosen_queries = select_rows(query_rows, dilation, head_count).reshape(
            -1, head_count, head_dim
        )
        keys_all = gathered[0].reshape(-1, head_count, head_dim)
        values_all = gathered[1].reshape(-1, head_count, head_dim)
        top, total, mixed = attend(chosen_queries, keys_all, values_all)
        member = jnp.asarray(row_ids[:, None] % dilation == (head_ids % dilation)[None, :])
        results.append(
            (
                repeat_rows(top, dilation, row_count),
                repeat_rows(total, dilation, row_count),
                repeat_rows(mixed, dilation, row_count),
                member,
            )
        )
    best = results[0][0]
    for item in results[1:]:
        best = jnp.maximum(best, jnp.where(item[3], item[0], best))
    numer = jnp.zeros((row_count, head_count, head_dim), jnp.float32)
    denom = jnp.zeros((row_count, head_count), jnp.float32)
    for item in results:
        factor = jnp.where(item[3], jnp.exp(jnp.where(item[3], item[0], best) - best), 0.0)
        numer = numer + factor[..., None] * item[2]
        denom = denom + factor * item[1]
    attended = (numer / denom[..., None]).reshape(row_count, feat_width).astype(jnp.bfloat16)
    projected = jnp.dot(
        attended,
        lax.all_gather(w_out, "grp", axis=0, tiled=True),
        preferred_element_type=jnp.float32,
    )
    return projected.astype(jnp.bfloat16)


def solution(mesh):
    placed = (P(("grp", "seq"), None), P(None, ("grp", "seq")), P(), P("grp", None))
    return jax.shard_map(
        shards, mesh=mesh, in_specs=placed, out_specs=P(("grp", "seq"), None), check_vma=False
    )
```

profile of v0, /device:TPU:1, one launch (start us, length us, event | category | flops | bytes accessed | tf_op | source)
XLA Modules:
  0.0 946.7 jit_solution(12771284679685522836)
XLA Ops:
  11.1 2.4 stack.31
  13.5 2.2 copy.155
  15.7 2.4 stack.30
  19.5 2.2 pad_maximum_fusion.1
  21.7 2.5 gather_fusion.1
  32.8 3.6 copy.171
  36.4 2.4 gather_fusion.5
  43.4 8.8 collective-permute-start
  52.2 2.4 stack.34
  54.6 2.3 stack.33
  61.7 2.4 gather_fusion.3
  67.0 43.4 %all_gather.13 = bf16[2,128,768]{2,0,1:T(2,128)(2,1)} all-gather(bf16[2,4,768]{2,0,1:T(2,128)(2,1)} %reshape.206), channel_id=1, replica_groups=mesh['grp'=16,'seq'=32] {'seq'}, dimensions={1}, use_global_device_ids=true | all-gather | bytes 405504 | tf_op jit(solution)/shard_map/all_gather | solution.py:87
  110.4 3.1 collective-permute-start.2
  116.4 2.1 collective-permute-start.1
  118.6 2.4 reshape.145
  120.9 2.3 reshape.142
  125.0 2.3 copy.161
  127.3 2.2 gather_fusion.2
  129.5 2.2 copy.153
  131.7 2.3 gather_fusion
  134.0 2.1 copy.168
  140.6 4.6 collective-permute-start.3
  148.0 2.3 copy.152
  150.4 2.4 fusion.74
  152.8 2.3 fusion.75
  156.4 2.0 fusion.77
  158.4 2.3 copy.176
  160.7 2.2 fusion.6
  162.9 2.5 convolution_bitcast_fusion.1
  171.2 2.8 broadcast_select_fusion.1
  174.0 3.9 slice_maximum_fusion
  177.9 4.7 copy.182
  182.6 4.6 copy.166
  192.0 2.4 reshape.153
  194.4 1.9 copy.184
  202.5 2.6 fusion.71
  205.2 2.3 copy.178
  207.4 2.3 copy.157
  213.6 2.4 reshape.152
  216.0 1.9 copy.180
  221.8 641.7 %all-gather.6.cloned.1.call-done = bf16[2,512,768]{2,0,1:T(2,128)(2,1)} async-done(((bf16[2,1,768]{2,0,1:T(2,128)(2,1)}), bf16[2,512,768]{2,0,1:T(2,128)(2,1)}) %all-gather.6.cloned.1.call-update) | async-done | bytes 1572880 | tf_op jit(solution)/shard_map/all_gather | solution.py:89
  863.5 5.7 fusion.70
  869.2 4.7 copy.197
  879.8 4.7 copy.198
  884.4 2.1 fusion.49
  893.5 2.0 fusion.20
  895.4 42.3 %all-gather.8.cloned.1.call-done = bf16[768,768]{1,0:T(8,128)(2,1)} async-done(((bf16[48,768]{1,0:T(8,128)(2,1)}), bf16[768,768]{1,0:T(8,128)(2,1)}) %all-gather.8.cloned.1.call-update) | async-done | bytes 1179664 | tf_op jit(solution)/shard_map/all_gather | solution.py:143
  937.8 2.4 convolution_convert_fusion.1
  (122 shorter events, 77.4 us)
Async XLA Ops:
  6.5 2.0 copy-start
  6.5 196.0 %all-gather.4.cloned.1.call-start = ((), (), s32[]{:S(2)}) async-start(), calls=%async_computation | async-start | bytes 1622016 | tf_op jit(solution)/shard_map/all_gather | solution.py:86
  18.1 3.7 copy-start.17
  27.5 836.0 %all-gather.6.cloned.1.call-start = ((), (), s32[]{:S(2)}) async-start(), calls=%async_computation.1 | async-start | bytes 1575936 | tf_op jit(solution)/shard_map/all_gather | solution.py:89
  41.5 896.2 %all-gather.8.cloned.1.call-start = ((), (), s32[]{:S(2)}) async-start(), calls=%async_computation.2 | async-start | bytes 1253376 | tf_op jit(solution)/shard_map/all_gather | solution.py:143
  43.4 70.1 %collective-permute-start = (bf16[2,128,768]{2,1,0:T(8,128)(2,1)}, bf16[2,128,768]{2,1,0:T(8,128)(2,1)}, u32[]{:S(2)}, u32[]{:S(2)}) collective-permute-start(bf16[2,128,768]{2,1,0:T(8,128)(2,1)} %pad_maximum_fusion.6), channel_id=1, source_target_pairs={{0,1},{1,0},{2,3},{3,2},{4,5},{5,4},{6,7},{7,6},{8,9},{9,8},{10,11... | collective-permute-start | bytes 1179656 | tf_op jit(solution)/shard_map/ppermute | solution.py:13
  110.4 27.0 %collective-permute-start.2 = (bf16[2,128,768]{2,0,1:T(2,128)(2,1)}, bf16[2,128,768]{2,0,1:T(2,128)(2,1)}, u32[]{:S(2)}, u32[]{:S(2)}) collective-permute-start(bf16[2,128,768]{2,0,1:T(2,128)(2,1)} %all_gather.13), channel_id=1, source_target_pairs={{0,32},{32,0},{64,96},{96,64},{128,160},{160,128},{192,224},{224,1... | collective-permute-start | bytes 1179656 | tf_op jit(solution)/shard_map/ppermute | solution.py:13
  114.7 0.7 copy-start.7
  114.7 1.7 copy-start.9
  116.4 28.8 %collective-permute-start.1 = (bf16[2,256,768]{2,1,0:T(8,128)(2,1)}, bf16[2,256,768]{2,1,0:T(8,128)(2,1)}, u32[]{:S(2)}, u32[]{:S(2)}) collective-permute-start(bf16[2,256,768]{2,1,0:T(8,128)(2,1)} %pad_maximum_fusion.4), channel_id=1, source_target_pairs={{0,2},{1,3},{2,0},{3,1},{4,6},{5,7},{6,4},{7,5},{8,10},{9,11},{10,... | collective-permute-start | bytes 2359304 | tf_op jit(solution)/shard_map/ppermute | solution.py:13
  137.4 7.8 copy-start.8
  137.4 7.8 copy-start.10
  138.7 8.0 copy-start.11
  138.7 8.0 copy-start.13
  140.6 30.7 %collective-permute-start.3 = (bf16[2,256,768]{2,0,1:T(2,128)(2,1)}, bf16[2,256,768]{2,0,1:T(2,128)(2,1)}, u32[]{:S(2)}, u32[]{:S(2)}) collective-permute-start(bf16[2,256,768]{2,0,1:T(2,128)(2,1)} %pad_maximum_fusion.5), channel_id=1, source_target_pairs={{0,64},{32,96},{64,0},{96,32},{128,192},{160,224},{192,128},{224,1... | collective-permute-start | bytes 2359304 | tf_op jit(solution)/shard_map/ppermute | solution.py:13
  150.4 4.7 copy-start.6
  150.4 4.7 copy-start.16
  155.0 13.1 %copy-start.18 = (f32[4,128]{1,0:T(4,128)}, f32[4,128]{1,0:T(4,128)S(1)}, u32[]{:S(2)}) copy-start(f32[4,128]{1,0:T(4,128)S(1)} %get-tuple-element.47) | copy-start | bytes 6148
  156.4 12.7 %copy-start.19 = (f32[4,128]{1,0:T(4,128)}, f32[4,128]{1,0:T(4,128)S(1)}, u32[]{:S(2)}) copy-start(f32[4,128]{1,0:T(4,128)S(1)} %get-tuple-element.49) | copy-start | bytes 6148
  160.7 4.7 copy-start.2
  162.9 3.4 copy-start.3
  162.9 4.3 copy-start.4
  162.9 4.3 copy-start.20
  165.4 2.7 copy-start.1
  169.1 2.1 copy-start.12
  169.1 2.1 copy-start.14
  209.7 2.4 copy-start.15
  211.3 0.8 copy-start.5
  869.2 6.9 copy-start.21
  869.2 6.9 copy-start.22
Sparse Core Ops, SparseCore 0:
  27.6 70.5 all-gather.3
  100.3 763.0 all-gather.5
  866.5 71.2 all-gather.7
where the time goes:
time: 950 us; the launch traced here: 947 us
  waiting for transfers between devices  684 us (72%)
  local copies, waits for them, and re-layouts  122 us (13%)
  blocking collectives  43.4 us (5%)
  other arithmetic  39.7 us (4%)
  matrix products  25.9 us (3%)
  starting transfers between devices  18.7 us (2%)
  between operations  13.4 us (1%)
    all_gather x1, waiting for transfers between devices, shards(): far_all = lax.all_gather(far_kv, ('grp', 'seq'), axis=1, tiled=True)  642 us
    all_gather x1, blocking collectives, shards(): lax.all_gather(third_kv, 'seq', axis=1, tiled=True)  43.4 us
    all_gather x1, waiting for transfers between devices, shards(): lax.all_gather(w_out, 'grp', axis=0, tiled=True)  42.3 us
    another operation x10, local copies, waits for them, and re-layouts, shards(): jnp.stack([qkv[:, feat_width:2 * feat_width], qkv[:, 2 * feat_width:]])  20.5 us
  transfers between devices with their start and end apart: 7, of which 2 were waited for; matrix products, arithmetic and copies ran while one was open for 17% of the time, Pallas kernels for 0%

commit v1 on v0

v1 whole, which is shorter than its diff:
```python
import jax
import jax.numpy as jnp
import numpy as np
from jax import lax
from jax.experimental import pallas as pl
from jax.experimental.pallas import tpu as pltpu
from jax.sharding import PartitionSpec as P

MESH = pl.DeviceIdType.MESH
F32 = jnp.float32
BF16 = jnp.bfloat16
ROWS = 128
WIDTH = 768
HEADS = 16
LOG2E = 1.4426950408889634
SCALE = 48 ** (-0.5) * LOG2E


def iota(shape, axis):
    return lax.broadcasted_iota(jnp.int32, shape, axis)


def dot(a, b):
    return jnp.dot(a, b, preferred_element_type=F32)


def dot_nt(a, b):
    return lax.dot_general(a, b, (((1,), (1,)), ((), ())), preferred_element_type=F32)


def row_order(p):
    return p // 16 + 8 * ((p % 4) * 4 + (p % 16) // 4)


def sine(angle, quarter_turns):
    turns = jnp.floor(angle * (2.0 / np.pi) + 0.5)
    rest = ((angle - turns * 1.5703125) - turns * 4.837512969970703125e-4) - turns * 7.54978995489188216e-8
    quadrant = turns.astype(jnp.int32) + quarter_turns
    sq = rest * rest
    sin_part = rest + rest * sq * (-1.6666654611e-1 + sq * (8.3321608736e-3 - sq * 1.9515295891e-4))
    cos_part = 1.0 - 0.5 * sq + sq * sq * (
        4.166664568298827e-2 + sq * (-1.388731625493765e-3 + sq * 2.443315711809948e-5)
    )
    value = jnp.where((quadrant & 1) == 1, cos_part, sin_part)
    return jnp.where((quadrant & 2) == 2, -value, value)


def soft(scores):
    top = jnp.max(scores, axis=1, keepdims=True)
    return top, jnp.exp2((scores - top) * SCALE)


def merge(a, l, b, m):
    gap = m - l
    share = 1.0 / (1.0 + jnp.exp2(-gap))
    both = jnp.maximum(l, m) + jnp.log2(1.0 + jnp.exp2(-jnp.abs(gap)))
    return a + (b - a) * share, both


def attend(queries, keys_values):
    top, weights = soft(dot_nt(queries, keys_values))
    mixed = dot(weights.astype(BF16), keys_values)
    total = mixed[:, 96:97]
    return mixed * (1.0 / total), top * SCALE + jnp.log2(total)


def kernel(
    tok_hbm, pos_hbm, omega_hbm, wqkv_hbm, wout_hbm, out_ref,
    tok, pos, omega, wq, emb, q_own, kv_all, msg, recv_a, kv3, far, q3, out2, msg_c, recv_c,
    att, lse, wall,
    load_sem, emb_send, emb_recv, a_send, a_recv, relay_send, relay_recv,
    kv3_send, kv3_recv, far_send, far_recv, o2_send, o2_recv, c_send, c_recv,
    w1_send, w1_recv, w2_send, w2_recv, w3_send, w3_recv,
):
    g = lax.axis_index("grp")
    s = lax.axis_index("seq")
    core = s % 2
    chip = s // 2
    x = s // 8
    zh = g // 4
    y = g % 4
    sibling = s + 1 - 2 * core
    across = s + 2 - 4 * (chip % 2)
    half_cols = pl.ds(pl.multiple_of(384 * core, 128), 384)

    def remote(src, dst, send_sem, recv_sem, grp, seq):
        return pltpu.make_async_remote_copy(
            src_ref=src, dst_ref=dst, send_sem=send_sem, recv_sem=recv_sem,
            device_id=(grp, seq), device_id_type=MESH,
        )

    def each(low, high, body):
        def step(i, carry):
            body(i)
            return carry
        lax.fori_loop(low, high, step, 0)

    load_tok = pltpu.make_async_copy(tok_hbm, tok, load_sem.at[0])
    load_pos = pltpu.make_async_copy(pos_hbm, pos, load_sem.at[1])
    load_omega = pltpu.make_async_copy(omega_hbm, omega, load_sem.at[2])
    load_wq = [
        pltpu.make_async_copy(
            wqkv_hbm.at[:, pl.ds(WIDTH * i, WIDTH)], wq.at[:, pl.ds(WIDTH * i, WIDTH)], load_sem.at[3 + i]
        )
        for i in range(3)
    ]
    load_tok.start()
    load_pos.start()
    load_omega.start()
    for item in load_wq:
        item.start()

    barrier = pltpu.get_barrier_semaphore()

    def greet(grp, seq):
        pl.semaphore_signal(barrier, inc=1, device_id=(grp, seq), device_id_type=MESH)

    @pl.when(core == 1)
    def _():
        each(1, 32, lambda k: greet(g, (s + k) % 32))
        each(1, 16, lambda k: greet((g + k) % 16, s))
        each(0, 9, lambda k: greet(zh * 4 + (y + 1 + k % 3) % 4, ((x + 1 + k // 3) % 4) * 8 + s % 8))

    @pl.when(core == 0)
    def _():
        each(0, 16, lambda k: greet(g, 2 * k + 1))
        greet(g, across)
        each(1, 4, lambda k: greet((g + 4 * k) % 16, s))
        each(1, 16, lambda k: greet(zh * 4 + (y + k % 4) % 4, ((x + k // 4) % 4) * 8 + s % 8))

    load_tok.wait()
    load_pos.wait()
    load_omega.wait()
    order = (row_order(iota((ROWS, ROWS), 0)) == iota((ROWS, ROWS), 1)).astype(F32)
    place = pos[...].astype(F32)
    pos_x = jnp.sum(order * place[0:1, :], axis=1, keepdims=True)
    pos_y = jnp.sum(order * place[1:2, :], axis=1, keepdims=True)
    order_bf = order.astype(BF16)
    for i in range(6):
        cols = slice(128 * i, 128 * i + 128)
        lane = iota((1, 128), 1) + 128 * i
        spot = pos_x if i < 3 else pos_y
        turn = ((lane % 384) >= 192).astype(jnp.int32)
        value = sine(spot * omega[0:1, cols], turn)
        emb[0, :, cols] = (dot(order_bf, tok[:, cols]) + value).astype(BF16)

    @pl.when(core == 1)
    def _():
        pl.semaphore_wait(barrier, 55)

    @pl.when(core == 0)
    def _():
        pl.semaphore_wait(barrier, 35)

    send_across = remote(emb.at[0], emb.at[2], emb_send.at[0], emb_recv.at[0], g, across)
    send_sibling = remote(emb.at[0], emb.at[1], emb_send.at[1], emb_recv.at[1], g, sibling)
    send_on = remote(emb.at[2], emb.at[3], emb_send.at[2], emb_recv.at[2], g, sibling)
    send_across.start()
    send_sibling.start()

    for i in range(3):
        load_wq[i].wait()
        for j in range(3):
            part = dot(emb[0], wq[:, WIDTH * i + 256 * j : WIDTH * i + 256 * j + 256]).astype(BF16)
            if i == 0:
                q_own[:, 256 * j : 256 * j + 256] = part
            else:
                first = WIDTH * (i - 1) + 256 * j
                kv_all[0:ROWS, first : first + 256] = part

    lane128 = iota((1, 128), 1)
    for rho in range(8):
        base = 128 * (rho >= 3)
        off = 48 * rho - base
        src_row = iota((256, 128), 0)
        dst_lane = iota((256, 128), 1)
        put_first = ((src_row == dst_lane + off) & (dst_lane < 48)).astype(F32).astype(BF16)
        put_second = (
            (src_row == dst_lane - 48 + off) & (dst_lane >= 48) & (dst_lane < 96)
        ).astype(F32).astype(BF16)
        rows = slice(16 * rho, 16 * rho + 16)
        for e in range(2):
            h = rho + 8 * e
            w0 = 384 * e + base
            q_part = dot(q_own[rows, w0 : w0 + 256], put_first)
            kv_part = dot(kv_all[rows, w0 : w0 + 256], put_first) + dot(
                kv_all[rows, WIDTH + w0 : WIDTH + w0 + 256], put_second
            )
            kv_part = jnp.where(lane128 >= 96, 1.0, kv_part)
            msg[h, :, 0:128] = kv_part.astype(BF16)
            msg[h, :, 128:256] = q_part.astype(BF16)

    def a_copy(k):
        h = (chip + k) % 16
        return remote(msg.at[h], recv_a.at[s], a_send.at[k], a_recv, g, 2 * h + 1)

    a_local = pltpu.make_async_copy(msg.at[chip], recv_a.at[s], a_recv)

    @pl.when(core == 1)
    def _():
        a_local.start()

    each(1, 16, lambda k: a_copy(k).start())

    @pl.when(core == 0)
    def _():
        a_copy(0).start()

    my_part = wall.at[zh, y, x % 3, :, half_cols]

    def w1_copy(k):
        return remote(my_part, my_part, w1_send.at[k], w1_recv.at[zh], (g + 4 * k) % 16, s)

    @pl.when(x < 3)
    def _():
        load = pltpu.make_async_copy(
            wout_hbm.at[pl.ds(pl.multiple_of(16 * (x % 3), 16), 16), half_cols], my_part, load_sem.at[6]
        )
        load.start()
        load.wait()
        each(1, 4, lambda k: w1_copy(k).start())

    def other_rows(slot):
        for j in range(6):
            cols = slice(256 * j, 256 * j + 256)
            kv_all[ROWS * slot : ROWS * slot + ROWS, cols] = dot(
                emb[slot], wq[:, WIDTH + 256 * j : WIDTH + 256 * j + 256]
            ).astype(BF16)

    send_sibling.wait_recv()
    other_rows(1)
    send_across.wait_recv()
    send_on.start()
    other_rows(2)
    send_on.wait_recv()
    other_rows(3)

    e_own = chip // 8
    relay = remote(recv_a, recv_a, relay_send, relay_recv, g, sibling)
    give = remote(out2, out2, o2_send, o2_recv, g, sibling)

    def kv3_copy(k):
        block = kv3.at[y]
        return remote(block, block, kv3_send.at[k], kv3_recv.at[y], zh * 4 + (y + k) % 4, s)

    def far_copy(k):
        return remote(
            kv3.at[y, pl.ds(0, 32)], far.at[g], far_send.at[k], far_recv.at[g],
            ((zh + k // 4) % 4) * 4 + k % 4, s,
        )

    @pl.when(core == 1)
    def _():
        pltpu.make_async_copy(recv_a, recv_a, a_recv).wait()
        relay.start()
        spot = iota((128, 512), 0)
        col = iota((128, 512), 1)
        pick = ((spot % 32) * 16 + 4 * e_own + spot // 32 == col).astype(F32).astype(BF16)
        chosen = dot(pick, recv_a[...].reshape(512, 256)).astype(BF16)
        kv3[y] = chosen[:, 0:128]
        q3[...] = chosen[:, 128:256]
        each(4, 16, lambda k: far_copy(k).start())
        each(1, 4, lambda k: kv3_copy(k).start())

    @pl.when(core == 0)
    def _():
        relay.wait_recv()

        def block(i, carry):
            rows = pl.ds(pl.multiple_of(128 * i, 128), 128)
            flat = recv_a[...].reshape(512, 256)
            queries = recv_a[pl.ds(8 * i, 8)][:, :, 128:256].reshape(128, 128)
            mixed, level = attend(queries, flat[:, 0:128])
            out2[rows, :] = jnp.where(lane128 < 48, level, mixed)
            return carry

        lax.fori_loop(0, 4, block, 0)
        give.start()

    def first_branch(rho, carry):
        b = (rho + 5) // 8
        off = 48 * rho - 128 * b
        lane = iota((1, 256), 1)
        mine = (lane >= off) & (lane < off + 48)
        keep = mine.astype(F32).astype(BF16)
        for e in range(2):
            w0 = 384 * e + 128 * b
            win = pl.ds(pl.multiple_of(w0, 128), 256)
            win_v = pl.ds(pl.multiple_of(WIDTH + w0, 128), 256)
            top, weights = soft(dot_nt(q_own[:, win] * keep, kv_all[:, win]))
            total = jnp.sum(weights, axis=1, keepdims=True)
            mixed = dot(weights.astype(BF16), kv_all[:, win_v]) * (1.0 / total)
            att[:, win] = jnp.where(mine, mixed, att[:, win])
            lse[rho + 8 * e] = jnp.broadcast_to(top * SCALE + jnp.log2(total), (ROWS, 128))
        return carry

    lax.fori_loop(0, 4, first_branch, 0)

    @pl.when(x < 3)
    def _():
        each(1, 4, lambda k: pltpu.make_async_copy(my_part, my_part, w1_recv.at[(zh + k) % 4]).wait())

    my_column = wall.at[:, y, x % 3, :, half_cols]

    def w2_copy(k):
        return remote(
            my_column, my_column, w2_send.at[k], w2_recv.at[(x % 3) * 4 + y],
            zh * 4 + (y + k % 4) % 4, ((x + k // 4) % 4) * 8 + s % 8,
        )

    @pl.when(x < 3)
    def _():
        each(1, 16, lambda k: w2_copy(k).start())

    def c_copy(k):
        there = (s + k) % 32
        return remote(msg_c.at[there], recv_c.at[chip], c_send.at[k], c_recv, g, there)

    @pl.when(core == 1)
    def _():
        each(1, 4, lambda k: pltpu.make_async_copy(kv3.at[0], kv3.at[0], kv3_recv.at[(y + k) % 4]).wait())
        mixed3, level3 = attend(q3[...], kv3[...].reshape(512, 128))
        each(4, 16, lambda k: pltpu.make_async_copy(
            far.at[0], far.at[0], far_recv.at[((zh + k // 4) % 4) * 4 + k % 4]).wait())
        for k in range(4):
            far[zh * 4 + k] = kv3[k, 0:32, :]
        mixed4, level4 = attend(q3[0:32, :], far[...].reshape(512, 128))
        give.wait_recv()
        for m in range(4):
            a, l = mixed3[32 * m : 32 * m + 32], level3[32 * m : 32 * m + 32]
            if m == 0:
                a, l = merge(a, l, mixed4, level4)
            rows = pl.ds(4 * e_own + m, 32, stride=16)
            held = out2[rows, :]
            a, l = merge(held, held[:, 0:1], a, l)
            out2[rows, :] = jnp.where(lane128 < 48, l, a)
        done = out2[...]
        level = done[:, 0:1]
        high = level.astype(BF16).astype(F32)
        mid = (level - high).astype(BF16).astype(F32)
        low = level - high - mid
        coded = jnp.where(lane128 == 0, high, jnp.where(lane128 == 1, mid, jnp.where(lane128 == 2, low, done)))
        msg_c[...] = coded.astype(BF16).reshape(32, 16, 128)
        pltpu.make_async_copy(msg_c.at[s], recv_c.at[chip], c_recv).start()
        each(1, 32, lambda k: c_copy(k).start())

    lax.fori_loop(4, 8, first_branch, 0)

    def from_plane(i):
        @pl.when(i != x * 4 + y)
        def _():
            pltpu.make_async_copy(my_column, my_column, w2_recv.at[i]).wait()

    each(0, 12, from_plane)
    w3 = remote(
        wall.at[:, :, :, :, half_cols], wall.at[:, :, :, :, half_cols], w3_send, w3_recv, g, sibling
    )
    w3.start()

    pltpu.make_async_copy(recv_c, recv_c, c_recv).wait()
    for rho in range(8):
        base = 128 * (rho >= 3)
        off = 48 * rho - base
        src_row = iota((128, 256), 0)
        dst_lane = iota((128, 256), 1)
        put_back = ((src_row - 48 + off == dst_lane) & (src_row >= 48) & (src_row < 96)).astype(F32).astype(BF16)
        add_up = (src_row < 3).astype(F32).astype(BF16)
        lane = iota((1, 256), 1)
        mine = (lane >= off) & (lane < off + 48)
        rows = slice(16 * rho, 16 * rho + 16)
        for e in range(2):
            h = rho + 8 * e
            w0 = 384 * e + base
            other = dot(recv_c[h], put_back)
            level = dot(recv_c[h], add_up)
            own_level = lse[h, rows, 0:1]
            held = att[rows, w0 : w0 + 256]
            share = 1.0 / (1.0 + jnp.exp2(own_level - level))
            att[rows, w0 : w0 + 256] = jnp.where(mine, held + (other - held) * share, held)

    back = (row_order(iota((ROWS, ROWS), 1)) == iota((ROWS, ROWS), 0)).astype(F32).astype(BF16)
    attended = dot(back, att[...].astype(BF16)).astype(BF16)
    w3.wait_recv()
    for j in range(3):
        cols = slice(256 * j, 256 * j + 256)
        out_ref[:, cols] = dot(attended, wall[:, :, :, :, cols].reshape(WIDTH, 256)).astype(BF16)

    send_across.wait_send()
    send_sibling.wait_send()
    send_on.wait_send()
    each(1, 16, lambda k: a_copy(k).wait_send())

    @pl.when(core == 0)
    def _():
        a_copy(0).wait_send()
        give.wait_send()

    @pl.when(core == 1)
    def _():
        relay.wait_send()
        each(1, 4, lambda k: kv3_copy(k).wait_send())
        each(4, 16, lambda k: far_copy(k).wait_send())
        each(1, 32, lambda k: c_copy(k).wait_send())

    @pl.when(x < 3)
    def _():
        each(1, 4, lambda k: w1_copy(k).wait_send())
        each(1, 16, lambda k: w2_copy(k).wait_send())

    w3.wait_send()


def shards(tokens, tile_pos, w_qkv, w_out):
    omega = 10000.0 ** (-(np.arange(WIDTH) % (WIDTH // 4)).astype(np.float64) / (WIDTH // 4))
    omega = jnp.asarray(np.broadcast_to(omega.astype(np.float32), (8, WIDTH)))
    dma = pltpu.SemaphoreType.DMA
    anywhere = pl.BlockSpec(memory_space=pl.ANY)
    return pl.pallas_call(
        kernel,
        out_shape=jax.ShapeDtypeStruct((ROWS, WIDTH), BF16),
        in_specs=[anywhere] * 5,
        out_specs=pl.BlockSpec(memory_space=pltpu.VMEM),
        scratch_shapes=[
            pltpu.VMEM((ROWS, WIDTH), BF16),
            pltpu.VMEM((2, ROWS), jnp.int32),
            pltpu.VMEM((8, WIDTH), F32),
            pltpu.VMEM((WIDTH, 3 * WIDTH), BF16),
            pltpu.VMEM((4, ROWS, WIDTH), BF16),
            pltpu.VMEM((ROWS, WIDTH), BF16),
            pltpu.VMEM((4 * ROWS, 2 * WIDTH), BF16),
            pltpu.VMEM((HEADS, 16, 256), BF16),
            pltpu.VMEM((32, 16, 256), BF16),
            pltpu.VMEM((4, 128, 128), BF16),
            pltpu.VMEM((16, 32, 128), BF16),
            pltpu.VMEM((128, 128), BF16),
            pltpu.VMEM((512, 128), F32),
            pltpu.VMEM((32, 16, 128), BF16),
            pltpu.VMEM((HEADS, 16, 128), BF16),
            pltpu.VMEM((ROWS, WIDTH), F32),
            pltpu.VMEM((HEADS, ROWS, 128), F32),
            pltpu.VMEM((4, 4, 3, 16, WIDTH), BF16),
            dma((7,)), dma((3,)), dma((3,)), dma((16,)), dma, dma, dma,
            dma((4,)), dma((4,)), dma((16,)), dma((16,)), dma, dma, dma((32,)), dma,
            dma((4,)), dma((4,)), dma((16,)), dma((12,)), dma, dma,
        ],
        compiler_params=pltpu.CompilerParams(
            collective_id=0, has_side_effects=True, vmem_limit_bytes=40 * 1024 * 1024
        ),
        name="dilated_attention",
    )(tokens, tile_pos, omega, w_qkv, w_out)


def solution(mesh):
    placed = (P(("grp", "seq"), None), P(None, ("grp", "seq")), P(), P("grp", None))
    return jax.shard_map(
        shards, mesh=mesh, in_specs=placed, out_specs=P(("grp", "seq"), None), check_vma=False
    )
```

time: 950 us -> 55.7 us (0.06)
  waiting for transfers between devices: 684 us -> 0 us
  local copies, waits for them, and re-layouts: 122 us -> 5.86 us
  Pallas kernels: 0 us -> 49.5 us
  blocking collectives: 43.4 us -> 0 us
  other arithmetic: 39.7 us -> 0 us
  matrix products: 25.9 us -> 0 us
  starting transfers between devices: 18.7 us -> 0 us
  between operations: 13.4 us -> 0.01 us
    all_gather x3 -> x0, waiting for transfers between devices: 684 us -> none  [the longest x1 642 us: shards(): far_all = lax.all_gather(far_kv, ('grp', 'seq'), axis=1, tiled=True)]
    pallas_call x0 -> x1, Pallas kernels: none -> 49.5 us  [shards(): pl.pallas_call(kernel, out_shape=jax.ShapeDtypeStruct((ROWS, WIDTH), BF16...]
    all_gather x1 -> x0, blocking collectives: 43.4 us -> none  [shards(): lax.all_gather(third_kv, 'seq', axis=1, tiled=True)]
    slice x11 -> x0, local copies, waits for them, and re-layouts: 32.1 us -> none  [the longest x3 12.7 us: shards(): values_all = gathered[1].reshape(-1, head_count, head_dim)]
    reshape x14 -> x0, local copies, waits for them, and re-layouts: 27.1 us -> none  [the longest x5 10 us: repeat_rows(): return shaped.reshape((row_count,) + block.shape[1:])]
    dot_general x16 -> x0, matrix products: 25.9 us -> none  [the longest x7 12.3 us: attend(): jnp.einsum('qhd,khd->hqk', queries, keys_all, preferred_element_type=jnp....]
    another operation x10 -> x1, local copies, waits for them, and re-layouts: 20.5 us -> 0.69 us  [shards(): jnp.stack([qkv[:, feat_width:2 * feat_width], qkv[:, 2 * feat_width:]])]
    ppermute x4 -> x0, starting transfers between devices: 18.6 us -> none  [swapped(): return lax.ppermute(value, axis, pairs)]
  transfers between devices with their start and end apart: 7 -> 0, of which waited for: 2 -> 0; matrix products, arithmetic and copies ran while one was open for 17% -> 0% of each run, Pallas kernels for 0% -> 0%
where the time goes in v1:
time: 55.7 us; the launch traced here: 55.4 us
  Pallas kernels  49.5 us (89%)
  local copies, waits for them, and re-layouts  5.86 us (11%)
    pallas_call x1, Pallas kernels, shards(): pl.pallas_call(kernel, out_shape=jax.ShapeDtypeStruct((ROWS, WIDTH), BF16...  49.5 us
    unnamed x9, local copies, waits for them, and re-layouts  5.17 us

profile of v1, /device:TPU:1, one launch (start us, length us, event | category | flops | bytes accessed | tf_op | source)
XLA Modules:
  0.0 55.4 jit_solution(2803770569335796189)
XLA Ops:
  0.0 0.7 %jit_solution_.3.omega_hbm = f32[8,768]{1,0:T(8,128)S(1)} broadcast(f32[768]{0:T(1024)} %constant.2.clone), dimensions={1} | broadcast | bytes 27648 | tf_op jit(solution)
  0.7 0.0 copy-start
  0.7 2.0 %copy-done = bf16[768,2304]{1,0:T(8,128)(2,1)S(1)} copy-done((bf16[768,2304]{1,0:T(8,128)(2,1)S(1)}, bf16[768,2304]{1,0:T(8,128)(2,1)}, u32[]{:S(2)}) %copy-start) | copy-done | bytes 3538968
  2.7 0.0 copy-start.1
  2.7 0.9 %copy-done.1 = bf16[128,768]{1,0:T(8,128)(2,1)S(1)} copy-done((bf16[128,768]{1,0:T(8,128)(2,1)S(1)}, bf16[128,768]{1,0:T(8,128)(2,1)}, u32[]{:S(2)}) %copy-start.1) | copy-done | bytes 196632
  3.6 0.0 copy-start.2
  3.6 0.9 %copy-done.2 = bf16[48,768]{1,0:T(8,128)(2,1)S(1)} copy-done((bf16[48,768]{1,0:T(8,128)(2,1)S(1)}, bf16[48,768]{1,0:T(8,128)(2,1)}, u32[]{:S(2)}) %copy-start.2) | copy-done | bytes 73752
  4.5 0.0 copy-start.3
  4.5 0.7 %copy-done.3 = s32[2,128]{1,0:T(2,128)S(1)} copy-done((s32[2,128]{1,0:T(2,128)S(1)}, s32[2,128]{1,0:T(2,128)}, u32[]{:S(2)}) %copy-start.3) | copy-done | bytes 1048
  5.2 49.5 %dilated_attention.1 = bf16[128,768]{1,0:T(8,128)(2,1)S(1)} custom-call(bf16[128,768]{1,0:T(8,128)(2,1)S(1)} %copy-done.1, s32[2,128]{1,0:T(2,128)S(1)} %copy-done.3, f32[8,768]{1,0:T(8,128)S(1)} %jit_solution_.3.omega_hbm, bf16[768,2304]{1,0:T(8,128)(2,1)S(1)} %copy-done, bf16[48,768]{1,0:T(8,128)(2,1)S(1)} %copy-done.2), custom_call_target="tpu_custom_call" | custom-call | tf_op jit(solution)/shard_map/dilated_attention/pallas_call | solution.py:418
  54.7 0.7 %copy.7 = bf16[128,768]{1,0:T(8,128)(2,1)} copy(bf16[128,768]{1,0:T(8,128)(2,1)S(1)} %dilated_attention.1) | data formatting | bytes 393216
Async XLA Ops:
  0.7 2.0 %copy-start = (bf16[768,2304]{1,0:T(8,128)(2,1)S(1)}, bf16[768,2304]{1,0:T(8,128)(2,1)}, u32[]{:S(2)}) copy-start(bf16[768,2304]{1,0:T(8,128)(2,1)} %wqkv_hbm.1) | copy-start | bytes 10616836
  2.7 0.9 %copy-start.1 = (bf16[128,768]{1,0:T(8,128)(2,1)S(1)}, bf16[128,768]{1,0:T(8,128)(2,1)}, u32[]{:S(2)}) copy-start(bf16[128,768]{1,0:T(8,128)(2,1)} %tok_hbm.1) | copy-start | bytes 589828
  3.6 0.9 %copy-start.2 = (bf16[48,768]{1,0:T(8,128)(2,1)S(1)}, bf16[48,768]{1,0:T(8,128)(2,1)}, u32[]{:S(2)}) copy-start(bf16[48,768]{1,0:T(8,128)(2,1)} %wout_hbm.1) | copy-start | bytes 221188
  4.5 0.7 %copy-start.3 = (s32[2,128]{1,0:T(2,128)S(1)}, s32[2,128]{1,0:T(2,128)}, u32[]{:S(2)}) copy-start(s32[2,128]{1,0:T(2,128)} %pos_hbm.1) | copy-start | bytes 3076

commit v2 on v1

--- a/solution.py
+++ b/solution.py
@@ -30,6 +30,14 @@
 
 def row_order(p):
     return p // 16 + 8 * ((p % 4) * 4 + (p % 16) // 4)
+
+
+def omega(lane):
+    j = lane % 192
+    rate = jnp.ones(lane.shape, F32)
+    for bit in range(8):
+        rate = jnp.where((j // 2**bit) % 2 == 1, rate * float(10000.0 ** (-(2**bit) / 192)), rate)
+    return rate
 
 
 def sine(angle, quarter_turns):
@@ -65,8 +73,8 @@
 
 
 def kernel(
-    tok_hbm, pos_hbm, omega_hbm, wqkv_hbm, wout_hbm, out_ref,
-    tok, pos, omega, wq, emb, q_own, kv_all, msg, recv_a, kv3, far, q3, out2, msg_c, recv_c,
+    tok_hbm, pos_hbm, wqkv_hbm, wout_hbm, out_ref,
+    tok, pos, wq, emb, q_own, kv_all, msg, recv_a, kv3, far, q3, out2, msg_c, recv_c,
     att, lse, wall,
     load_sem, emb_send, emb_recv, a_send, a_recv, relay_send, relay_recv,
     kv3_send, kv3_recv, far_send, far_recv, o2_send, o2_recv, c_send, c_recv,
@@ -97,16 +105,14 @@
 
     load_tok = pltpu.make_async_copy(tok_hbm, tok, load_sem.at[0])
     load_pos = pltpu.make_async_copy(pos_hbm, pos, load_sem.at[1])
-    load_omega = pltpu.make_async_copy(omega_hbm, omega, load_sem.at[2])
     load_wq = [
         pltpu.make_async_copy(
-            wqkv_hbm.at[:, pl.ds(WIDTH * i, WIDTH)], wq.at[:, pl.ds(WIDTH * i, WIDTH)], load_sem.at[3 + i]
+            wqkv_hbm.at[:, pl.ds(WIDTH * i, WIDTH)], wq.at[:, pl.ds(WIDTH * i, WIDTH)], load_sem.at[2 + i]
         )
         for i in range(3)
     ]
     load_tok.start()
     load_pos.start()
-    load_omega.start()
     for item in load_wq:
         item.start()
 
@@ -130,7 +136,6 @@
 
     load_tok.wait()
     load_pos.wait()
-    load_omega.wait()
     order = (row_order(iota((ROWS, ROWS), 0)) == iota((ROWS, ROWS), 1)).astype(F32)
     place = pos[...].astype(F32)
     pos_x = jnp.sum(order * place[0:1, :], axis=1, keepdims=True)
@@ -141,7 +146,7 @@
         lane = iota((1, 128), 1) + 128 * i
         spot = pos_x if i < 3 else pos_y
         turn = ((lane % 384) >= 192).astype(jnp.int32)
-        value = sine(spot * omega[0:1, cols], turn)
+        value = sine(spot * omega(lane), turn)
         emb[0, :, cols] = (dot(order_bf, tok[:, cols]) + value).astype(BF16)
 
     @pl.when(core == 1)
@@ -214,7 +219,7 @@
     @pl.when(x < 3)
     def _():
         load = pltpu.make_async_copy(
-            wout_hbm.at[pl.ds(pl.multiple_of(16 * (x % 3), 16), 16), half_cols], my_part, load_sem.at[6]
+            wout_hbm.at[pl.ds(pl.multiple_of(16 * (x % 3), 16), 16), half_cols], my_part, load_sem.at[5]
         )
         load.start()
         load.wait()
@@ -411,19 +416,16 @@
 
 
 def shards(tokens, tile_pos, w_qkv, w_out):
-    omega = 10000.0 ** (-(np.arange(WIDTH) % (WIDTH // 4)).astype(np.float64) / (WIDTH // 4))
-    omega = jnp.asarray(np.broadcast_to(omega.astype(np.float32), (8, WIDTH)))
     dma = pltpu.SemaphoreType.DMA
-    anywhere = pl.BlockSpec(memory_space=pl.ANY)
+    in_hbm = pl.BlockSpec(memory_space=pltpu.HBM)
     return pl.pallas_call(
         kernel,
         out_shape=jax.ShapeDtypeStruct((ROWS, WIDTH), BF16),
-        in_specs=[anywhere] * 5,
+        in_specs=[in_hbm] * 4,
         out_specs=pl.BlockSpec(memory_space=pltpu.VMEM),
         scratch_shapes=[
             pltpu.VMEM((ROWS, WIDTH), BF16),
             pltpu.VMEM((2, ROWS), jnp.int32),
-            pltpu.VMEM((8, WIDTH), F32),
             pltpu.VMEM((WIDTH, 3 * WIDTH), BF16),
             pltpu.VMEM((4, ROWS, WIDTH), BF16),
             pltpu.VMEM((ROWS, WIDTH), BF16),
@@ -439,15 +441,15 @@
             pltpu.VMEM((ROWS, WIDTH), F32),
             pltpu.VMEM((HEADS, ROWS, 128), F32),
             pltpu.VMEM((4, 4, 3, 16, WIDTH), BF16),
-            dma((7,)), dma((3,)), dma((3,)), dma((16,)), dma, dma, dma,
+            dma((6,)), dma((3,)), dma((3,)), dma((16,)), dma, dma, dma,
             dma((4,)), dma((4,)), dma((16,)), dma((16,)), dma, dma, dma((32,)), dma,
             dma((4,)), dma((4,)), dma((16,)), dma((12,)), dma, dma,
         ],
         compiler_params=pltpu.CompilerParams(
-            collective_id=0, has_side_effects=True, vmem_limit_bytes=40 * 1024 * 1024
+            collective_id=0, has_side_effects=True, vmem_limit_bytes=60 * 1024 * 1024
         ),
         name="dilated_attention",
-    )(tokens, tile_pos, omega, w_qkv, w_out)
+    )(tokens, tile_pos, w_qkv, w_out)
 
 
 def solution(mesh):

time: 55.7 us -> 51.5 us (0.925)
  local copies, waits for them, and re-layouts: 5.86 us -> 1.62 us
    unnamed x9 -> x1, local copies, waits for them, and re-layouts: 5.17 us -> 1.62 us
    another operation x1 -> x0, local copies, waits for them, and re-layouts: 0.69 us -> none
where the time goes in v2:
time: 51.5 us; the launch traced here: 51.3 us
  Pallas kernels  49.7 us (97%)
  local copies, waits for them, and re-layouts  1.62 us (3%)
    pallas_call x1, Pallas kernels, shards(): pl.pallas_call(kernel, out_shape=jax.ShapeDtypeStruct((ROWS, WIDTH), BF16...  49.7 us
    unnamed x1, local copies, waits for them, and re-layouts  1.62 us

profile of v2, /device:TPU:1, one launch (start us, length us, event | category | flops | bytes accessed | tf_op | source)
XLA Modules:
  0.0 51.3 jit_solution(415208919540123255)
XLA Ops:
  0.0 49.7 %dilated_attention.1 = bf16[128,768]{1,0:T(8,128)(2,1)} custom-call(bf16[128,768]{1,0:T(8,128)(2,1)} %tok_hbm.1, s32[2,128]{1,0:T(2,128)} %pos_hbm.1, bf16[768,2304]{1,0:T(8,128)(2,1)} %wqkv_hbm.1, bf16[48,768]{1,0:T(8,128)(2,1)} %wout_hbm.1), custom_call_target="tpu_custom_call" | custom-call | tf_op jit(solution)/shard_map/dilated_attention/pallas_call | solution.py:421
  49.7 1.6 %copy.6 = bf16[128,768]{1,0:T(8,128)(2,1)} copy(bf16[128,768]{1,0:T(8,128)(2,1)} %dilated_attention.1) | data formatting | bytes 393216

commit v3 on v2

--- a/solution.py
+++ b/solution.py
@@ -78,7 +78,7 @@
     att, lse, wall,
     load_sem, emb_send, emb_recv, a_send, a_recv, relay_send, relay_recv,
     kv3_send, kv3_recv, far_send, far_recv, o2_send, o2_recv, c_send, c_recv,
-    w1_send, w1_recv, w2_send, w2_recv, w3_send, w3_recv,
+    w1_send, w1_recv, w2_send, w2_recv, w3_send, w3_recv, past, past_too,
 ):
     g = lax.axis_index("grp")
     s = lax.axis_index("seq")
@@ -102,6 +102,9 @@
             body(i)
             return carry
         lax.fori_loop(low, high, step, 0)
+
+    def seat(k):
+        return ((x + 2 + k // 4) % 4) * 4 + (chip + k) % 4
 
     load_tok = pltpu.make_async_copy(tok_hbm, tok, load_sem.at[0])
     load_pos = pltpu.make_async_copy(pos_hbm, pos, load_sem.at[1])
@@ -116,6 +119,15 @@
     for item in load_wq:
         item.start()
 
+    my_part = wall.at[zh, y, x % 3, :, half_cols]
+    load_wout = pltpu.make_async_copy(
+        wout_hbm.at[pl.ds(pl.multiple_of(16 * (x % 3), 16), 16), half_cols], my_part, load_sem.at[5]
+    )
+
+    @pl.when(x < 3)
+    def _():
+        load_wout.start()
+
     barrier = pltpu.get_barrier_semaphore()
 
     def greet(grp, seq):
@@ -123,15 +135,17 @@
 
     @pl.when(core == 1)
     def _():
+        greet((g + 4) % 16, s)
+        greet((g + 12) % 16, s)
         each(1, 32, lambda k: greet(g, (s + k) % 32))
-        each(1, 16, lambda k: greet((g + k) % 16, s))
-        each(0, 9, lambda k: greet(zh * 4 + (y + 1 + k % 3) % 4, ((x + 1 + k // 3) % 4) * 8 + s % 8))
+        each(1, 4, lambda k: greet(zh * 4 + (y + k) % 4, s))
 
     @pl.when(core == 0)
     def _():
+        greet((g + 4) % 16, s)
+        greet((g + 12) % 16, s)
         each(0, 16, lambda k: greet(g, 2 * k + 1))
         greet(g, across)
-        each(1, 4, lambda k: greet((g + 4 * k) % 16, s))
         each(1, 16, lambda k: greet(zh * 4 + (y + k % 4) % 4, ((x + k // 4) % 4) * 8 + s % 8))
 
     load_tok.wait()
@@ -148,20 +162,6 @@
         turn = ((lane % 384) >= 192).astype(jnp.int32)
         value = sine(spot * omega(lane), turn)
         emb[0, :, cols] = (dot(order_bf, tok[:, cols]) + value).astype(BF16)
-
-    @pl.when(core == 1)
-    def _():
-        pl.semaphore_wait(barrier, 55)
-
-    @pl.when(core == 0)
-    def _():
-        pl.semaphore_wait(barrier, 35)
-
-    send_across = remote(emb.at[0], emb.at[2], emb_send.at[0], emb_recv.at[0], g, across)
-    send_sibling = remote(emb.at[0], emb.at[1], emb_send.at[1], emb_recv.at[1], g, sibling)
-    send_on = remote(emb.at[2], emb.at[3], emb_send.at[2], emb_recv.at[2], g, sibling)
-    send_across.start()
-    send_sibling.start()
 
     for i in range(3):
         load_wq[i].wait()
@@ -195,35 +195,58 @@
             msg[h, :, 0:128] = kv_part.astype(BF16)
             msg[h, :, 128:256] = q_part.astype(BF16)
 
+    @pl.when(core == 1)
+    def _():
+        pl.semaphore_wait(barrier, 36)
+
+    @pl.when(core == 0)
+    def _():
+        pl.semaphore_wait(barrier, 34)
+
     def a_copy(k):
-        h = (chip + k) % 16
+        h = seat(k)
         return remote(msg.at[h], recv_a.at[s], a_send.at[k], a_recv, g, 2 * h + 1)
 
     a_local = pltpu.make_async_copy(msg.at[chip], recv_a.at[s], a_recv)
 
+    def a_all(act):
+        each(0, 8, lambda k: act(a_copy(k)))
+        each(9, 16, lambda k: act(a_copy(k)))
+
+        @pl.when(core == 0)
+        def _():
+            act(a_copy(8))
+
+    a_all(lambda c: c.start())
+
     @pl.when(core == 1)
     def _():
         a_local.start()
 
-    each(1, 16, lambda k: a_copy(k).start())
-
-    @pl.when(core == 0)
-    def _():
-        a_copy(0).start()
-
-    my_part = wall.at[zh, y, x % 3, :, half_cols]
+    send_across = remote(emb.at[0], emb.at[2], emb_send.at[0], emb_recv.at[0], g, across)
+    send_sibling = remote(emb.at[0], emb.at[1], emb_send.at[1], emb_recv.at[1], g, sibling)
+    send_on = remote(emb.at[2], emb.at[3], emb_send.at[2], emb_recv.at[2], g, sibling)
+    send_across.start()
+    send_sibling.start()
+
+    def tell(sem, grp):
+        pl.semaphore_signal(sem, inc=1, device_id=(grp, s), device_id_type=MESH)
+
+    tell(past, (g + 12) % 16)
+
+    @pl.when(core == 1)
+    def _():
+        each(1, 4, lambda k: tell(past, zh * 4 + (y + k) % 4))
+
 
     def w1_copy(k):
         return remote(my_part, my_part, w1_send.at[k], w1_recv.at[zh], (g + 4 * k) % 16, s)
 
     @pl.when(x < 3)
     def _():
-        load = pltpu.make_async_copy(
-            wout_hbm.at[pl.ds(pl.multiple_of(16 * (x % 3), 16), 16), half_cols], my_part, load_sem.at[5]
-        )
-        load.start()
-        load.wait()
-        each(1, 4, lambda k: w1_copy(k).start())
+        load_wout.wait()
+        w1_copy(1).start()
+        w1_copy(3).start()
 
     def other_rows(slot):
         for j in range(6):
@@ -234,11 +257,19 @@
 
     send_sibling.wait_recv()
     other_rows(1)
-    send_across.wait_recv()
-    send_on.start()
-    other_rows(2)
-    send_on.wait_recv()
-    other_rows(3)
+
+    @pl.when(core == 1)
+    def _():
+        pl.semaphore_wait(past, 4)
+        each(1, 4, lambda k: tell(past_too, zh * 4 + (y + k) % 4))
+
+    @pl.when(core == 0)
+    def _():
+        pl.semaphore_wait(past, 1)
+
+    @pl.when(x < 3)
+    def _():
+        w1_copy(2).start()
 
     e_own = chip // 8
     relay = remote(recv_a, recv_a, relay_send, relay_recv, g, sibling)
@@ -251,8 +282,11 @@
     def far_copy(k):
         return remote(
             kv3.at[y, pl.ds(0, 32)], far.at[g], far_send.at[k], far_recv.at[g],
-            ((zh + k // 4) % 4) * 4 + k % 4, s,
+            ((zh + far_step(k)) % 4) * 4 + (y + 2 + k) % 4, s,
         )
+
+    def far_step(k):
+        return (k // 4) % 3 + 1
 
     @pl.when(core == 1)
     def _():
@@ -264,6 +298,7 @@
         chosen = dot(pick, recv_a[...].reshape(512, 256)).astype(BF16)
         kv3[y] = chosen[:, 0:128]
         q3[...] = chosen[:, 128:256]
+        pl.semaphore_wait(past_too, 3)
         each(4, 16, lambda k: far_copy(k).start())
         each(1, 4, lambda k: kv3_copy(k).start())
 
@@ -281,6 +316,12 @@
 
         lax.fori_loop(0, 4, block, 0)
         give.start()
+
+    send_across.wait_recv()
+    send_on.start()
+    other_rows(2)
+    send_on.wait_recv()
+    other_rows(3)
 
     def first_branch(rho, carry):
         b = (rho + 5) // 8
@@ -318,27 +359,33 @@
         each(1, 16, lambda k: w2_copy(k).start())
 
     def c_copy(k):
-        there = (s + k) % 32
+        there = 2 * seat(k // 2) + 1 - k % 2
         return remote(msg_c.at[there], recv_c.at[chip], c_send.at[k], c_recv, g, there)
+
+    def c_all(act):
+        each(0, 16, lambda k: act(c_copy(k)))
+        each(17, 32, lambda k: act(c_copy(k)))
 
     @pl.when(core == 1)
     def _():
         each(1, 4, lambda k: pltpu.make_async_copy(kv3.at[0], kv3.at[0], kv3_recv.at[(y + k) % 4]).wait())
         mixed3, level3 = attend(q3[...], kv3[...].reshape(512, 128))
-        each(4, 16, lambda k: pltpu.make_async_copy(
-            far.at[0], far.at[0], far_recv.at[((zh + k // 4) % 4) * 4 + k % 4]).wait())
-        for k in range(4):
-            far[zh * 4 + k] = kv3[k, 0:32, :]
-        mixed4, level4 = attend(q3[0:32, :], far[...].reshape(512, 128))
         give.wait_recv()
-        for m in range(4):
-            a, l = mixed3[32 * m : 32 * m + 32], level3[32 * m : 32 * m + 32]
-            if m == 0:
-                a, l = merge(a, l, mixed4, level4)
+
+        def fold(m, a, l):
             rows = pl.ds(4 * e_own + m, 32, stride=16)
             held = out2[rows, :]
             a, l = merge(held, held[:, 0:1], a, l)
             out2[rows, :] = jnp.where(lane128 < 48, l, a)
+
+        for m in range(4):
+            fold(m, mixed3[32 * m : 32 * m + 32], level3[32 * m : 32 * m + 32])
+        for k in range(4):
+            far[zh * 4 + k] = kv3[k, 0:32, :]
+        each(4, 16, lambda k: pltpu.make_async_copy(
+            far.at[0], far.at[0], far_recv.at[((zh + k // 4) % 4) * 4 + k % 4]).wait())
+        mixed4, level4 = attend(q3[0:32, :], far[...].reshape(512, 128))
+        fold(0, mixed4, level4)
         done = out2[...]
         level = done[:, 0:1]
         high = level.astype(BF16).astype(F32)
@@ -346,21 +393,25 @@
         low = level - high - mid
         coded = jnp.where(lane128 == 0, high, jnp.where(lane128 == 1, mid, jnp.where(lane128 == 2, low, done)))
         msg_c[...] = coded.astype(BF16).reshape(32, 16, 128)
+        c_all(lambda c: c.start())
         pltpu.make_async_copy(msg_c.at[s], recv_c.at[chip], c_recv).start()
-        each(1, 32, lambda k: c_copy(k).start())
 
     lax.fori_loop(4, 8, first_branch, 0)
 
-    def from_plane(i):
-        @pl.when(i != x * 4 + y)
-        def _():
-            pltpu.make_async_copy(my_column, my_column, w2_recv.at[i]).wait()
-
-    each(0, 12, from_plane)
-    w3 = remote(
-        wall.at[:, :, :, :, half_cols], wall.at[:, :, :, :, half_cols], w3_send, w3_recv, g, sibling
-    )
-    w3.start()
+    def w3_part(i):
+        piece = wall.at[:, :, i, :, half_cols]
+        return remote(piece, piece, w3_send.at[i], w3_recv.at[i], g, sibling)
+
+    def w3_start(i):
+        def from_plane(j):
+            @pl.when((i != x) | (j != y))
+            def _():
+                pltpu.make_async_copy(my_column, my_column, w2_recv.at[i * 4 + j]).wait()
+
+        each(0, 4, from_plane)
+        w3_part(i).start()
+
+    each(0, 3, w3_start)
 
     pltpu.make_async_copy(recv_c, recv_c, c_recv).wait()
     for rho in range(8):
@@ -385,7 +436,7 @@
 
     back = (row_order(iota((ROWS, ROWS), 1)) == iota((ROWS, ROWS), 0)).astype(F32).astype(BF16)
     attended = dot(back, att[...].astype(BF16)).astype(BF16)
-    w3.wait_recv()
+    each(0, 3, lambda i: w3_part(i).wait_recv())
     for j in range(3):
         cols = slice(256 * j, 256 * j + 256)
         out_ref[:, cols] = dot(attended, wall[:, :, :, :, cols].reshape(WIDTH, 256)).astype(BF16)
@@ -393,11 +444,10 @@
     send_across.wait_send()
     send_sibling.wait_send()
     send_on.wait_send()
-    each(1, 16, lambda k: a_copy(k).wait_send())
+    a_all(lambda c: c.wait_send())
 
     @pl.when(core == 0)
     def _():
-        a_copy(0).wait_send()
         give.wait_send()
 
     @pl.when(core == 1)
@@ -405,14 +455,14 @@
         relay.wait_send()
         each(1, 4, lambda k: kv3_copy(k).wait_send())
         each(4, 16, lambda k: far_copy(k).wait_send())
-        each(1, 32, lambda k: c_copy(k).wait_send())
+        c_all(lambda c: c.wait_send())
 
     @pl.when(x < 3)
     def _():
         each(1, 4, lambda k: w1_copy(k).wait_send())
         each(1, 16, lambda k: w2_copy(k).wait_send())
 
-    w3.wait_send()
+    each(0, 3, lambda i: w3_part(i).wait_send())
 
 
 def shards(tokens, tile_pos, w_qkv, w_out):
@@ -443,7 +493,8 @@
             pltpu.VMEM((4, 4, 3, 16, WIDTH), BF16),
             dma((6,)), dma((3,)), dma((3,)), dma((16,)), dma, dma, dma,
             dma((4,)), dma((4,)), dma((16,)), dma((16,)), dma, dma, dma((32,)), dma,
-            dma((4,)), dma((4,)), dma((16,)), dma((12,)), dma, dma,
+            dma((4,)), dma((4,)), dma((16,)), dma((12,)), dma((3,)), dma((3,)),
+            pltpu.SemaphoreType.REGULAR, pltpu.SemaphoreType.REGULAR,
         ],
         compiler_params=pltpu.CompilerParams(
             collective_id=0, has_side_effects=True, vmem_limit_bytes=60 * 1024 * 1024

time: 51.5 us -> 49.9 us (0.969)
  Pallas kernels: 49.7 us -> 48.1 us
    pallas_call x1, Pallas kernels: 49.7 us -> 48.1 us  [shards(): pl.pallas_call(kernel, out_shape=jax.ShapeDtypeStruct((ROWS, WIDTH), BF16...]
where the time goes in v3:
time: 49.9 us; the launch traced here: 49.8 us
  Pallas kernels  48.1 us (96%)
  local copies, waits for them, and re-layouts  1.62 us (3%)
    pallas_call x1, Pallas kernels, shards(): pl.pallas_call(kernel, out_shape=jax.ShapeDtypeStruct((ROWS, WIDTH), BF16...  48.1 us
    unnamed x1, local copies, waits for them, and re-layouts  1.62 us

profile of v3, /device:TPU:1, one launch (start us, length us, event | category | flops | bytes accessed | tf_op | source)
XLA Modules:
  0.0 49.8 jit_solution(2554524656065079333)
XLA Ops:
  0.0 48.1 %dilated_attention.1 = bf16[128,768]{1,0:T(8,128)(2,1)} custom-call(bf16[128,768]{1,0:T(8,128)(2,1)} %tok_hbm.1, s32[2,128]{1,0:T(2,128)} %pos_hbm.1, bf16[768,2304]{1,0:T(8,128)(2,1)} %wqkv_hbm.1, bf16[48,768]{1,0:T(8,128)(2,1)} %wout_hbm.1), custom_call_target="tpu_custom_call" | custom-call | tf_op jit(solution)/shard_map/dilated_attention/pallas_call | solution.py:471
  48.1 1.6 %copy.6 = bf16[128,768]{1,0:T(8,128)(2,1)} copy(bf16[128,768]{1,0:T(8,128)(2,1)} %dilated_attention.1) | data formatting | bytes 393216

commit v4 on v3

--- a/solution.py
+++ b/solution.py
@@ -89,7 +89,7 @@
     y = g % 4
     sibling = s + 1 - 2 * core
     across = s + 2 - 4 * (chip % 2)
-    half_cols = pl.ds(pl.multiple_of(384 * core, 128), 384)
+    sender = (core == 0) & (x < 3)
 
     def remote(src, dst, send_sem, recv_sem, grp, seq):
         return pltpu.make_async_remote_copy(
@@ -119,12 +119,12 @@
     for item in load_wq:
         item.start()
 
-    my_part = wall.at[zh, y, x % 3, :, half_cols]
+    my_block = (zh * 4 + y) * 3 + x % 3
     load_wout = pltpu.make_async_copy(
-        wout_hbm.at[pl.ds(pl.multiple_of(16 * (x % 3), 16), 16), half_cols], my_part, load_sem.at[5]
+        wout_hbm.at[pl.ds(pl.multiple_of(16 * (x % 3), 16), 16)], wall.at[my_block], load_sem.at[5]
     )
 
-    @pl.when(x < 3)
+    @pl.when(sender)
     def _():
         load_wout.start()
 
@@ -232,21 +232,59 @@
     def tell(sem, grp):
         pl.semaphore_signal(sem, inc=1, device_id=(grp, s), device_id_type=MESH)
 
-    tell(past, (g + 12) % 16)
-
-    @pl.when(core == 1)
-    def _():
+    @pl.when(core == 1)
+    def _():
+        tell(past, (g + 12) % 16)
         each(1, 4, lambda k: tell(past, zh * 4 + (y + k) % 4))
 
-
-    def w1_copy(k):
-        return remote(my_part, my_part, w1_send.at[k], w1_recv.at[zh], (g + 4 * k) % 16, s)
-
-    @pl.when(x < 3)
+    def block_of(step):
+        return (((zh + step) % 4) * 4 + y) * 3 + x % 3
+
+    def w1_copy(k, step):
+        block = wall.at[block_of(step)]
+        return remote(
+            block, block, w1_send.at[k + step], w1_recv.at[(zh + step) % 4], (g + 4 * k + 16) % 16, s
+        )
+
+    def w1_wait(step):
+        block = wall.at[block_of(step)]
+        pltpu.make_async_copy(block, block, w1_recv.at[(zh + step) % 4]).wait()
+
+    def w2_copy(k, step):
+        block = wall.at[block_of(step)]
+        return remote(
+            block, block, w2_send.at[step, k], w2_recv.at[(zh + step) % 4],
+            zh * 4 + (y + k % 4) % 4, ((x + k // 4) % 4) * 8 + s % 8,
+        )
+
+    def w2_start(step):
+        each(1, 16, lambda k: w2_copy(k, step).start())
+
+    def w2_wait(step):
+        sem = w2_recv.at[(zh + step) % 4]
+
+        @pl.when(x < 3)
+        def _():
+            pltpu.make_async_copy(wall.at[pl.ds(0, 11)], wall.at[pl.ds(0, 11)], sem).wait()
+
+        @pl.when(x == 3)
+        def _():
+            pltpu.make_async_copy(wall.at[pl.ds(0, 12)], wall.at[pl.ds(0, 12)], sem).wait()
+
+    def w3_copy(i):
+        blocks = wall.at[pl.ds(12 * i, 12)]
+        return remote(blocks, blocks, w3_send.at[i], w3_recv.at[i], g, sibling)
+
+    def w3_start(step):
+        w2_wait(step)
+        w3_copy((zh + step) % 4).start()
+
+    @pl.when(sender)
     def _():
         load_wout.wait()
-        w1_copy(1).start()
-        w1_copy(3).start()
+        w1_copy(1, 0).start()
+        w1_copy(3, 0).start()
+        w2_start(0)
 
     def other_rows(slot):
         for j in range(6):
@@ -263,13 +301,13 @@
         pl.semaphore_wait(past, 4)
         each(1, 4, lambda k: tell(past_too, zh * 4 + (y + k) % 4))
 
-    @pl.when(core == 0)
-    def _():
-        pl.semaphore_wait(past, 1)
-
-    @pl.when(x < 3)
-    def _():
-        w1_copy(2).start()
+    @pl.when(sender)
+    def _():
+        w1_wait(1)
+        w1_copy(3, 1).start()
+        w1_wait(3)
+        w2_start(1)
+        w2_start(3)
 
     e_own = chip // 8
     relay = remote(recv_a, recv_a, relay_send, relay_recv, g, sibling)
@@ -316,6 +354,11 @@
 
         lax.fori_loop(0, 4, block, 0)
         give.start()
+
+    @pl.when(sender)
+    def _():
+        w1_wait(2)
+        w2_start(2)
 
     send_across.wait_recv()
     send_on.start()
@@ -342,21 +385,11 @@
 
     lax.fori_loop(0, 4, first_branch, 0)
 
-    @pl.when(x < 3)
-    def _():
-        each(1, 4, lambda k: pltpu.make_async_copy(my_part, my_part, w1_recv.at[(zh + k) % 4]).wait())
-
-    my_column = wall.at[:, y, x % 3, :, half_cols]
-
-    def w2_copy(k):
-        return remote(
-            my_column, my_column, w2_send.at[k], w2_recv.at[(x % 3) * 4 + y],
-            zh * 4 + (y + k % 4) % 4, ((x + k // 4) % 4) * 8 + s % 8,
-        )
-
-    @pl.when(x < 3)
-    def _():
-        each(1, 16, lambda k: w2_copy(k).start())
+    @pl.when(core == 0)
+    def _():
+        w3_start(0)
+        w3_start(1)
+        w3_start(3)
 
     def c_copy(k):
         there = 2 * seat(k // 2) + 1 - k % 2
@@ -398,20 +431,9 @@
 
     lax.fori_loop(4, 8, first_branch, 0)
 
-    def w3_part(i):
-        piece = wall.at[:, :, i, :, half_cols]
-        return remote(piece, piece, w3_send.at[i], w3_recv.at[i], g, sibling)
-
-    def w3_start(i):
-        def from_plane(j):
-            @pl.when((i != x) | (j != y))
-            def _():
-                pltpu.make_async_copy(my_column, my_column, w2_recv.at[i * 4 + j]).wait()
-
-        each(0, 4, from_plane)
-        w3_part(i).start()
-
-    each(0, 3, w3_start)
+    @pl.when(core == 0)
+    def _():
+        w3_start(2)
 
     pltpu.make_async_copy(recv_c, recv_c, c_recv).wait()
     for rho in range(8):
@@ -436,10 +458,14 @@
 
     back = (row_order(iota((ROWS, ROWS), 1)) == iota((ROWS, ROWS), 0)).astype(F32).astype(BF16)
     attended = dot(back, att[...].astype(BF16)).astype(BF16)
-    each(0, 3, lambda i: w3_part(i).wait_recv())
+
+    @pl.when(core == 1)
+    def _():
+        each(0, 4, lambda i: w3_copy(i).wait_recv())
+
     for j in range(3):
         cols = slice(256 * j, 256 * j + 256)
-        out_ref[:, cols] = dot(attended, wall[:, :, :, :, cols].reshape(WIDTH, 256)).astype(BF16)
+        out_ref[:, cols] = dot(attended, wall[:, :, cols].reshape(WIDTH, 256)).astype(BF16)
 
     send_across.wait_send()
     send_sibling.wait_send()
@@ -457,12 +483,17 @@
         each(4, 16, lambda k: far_copy(k).wait_send())
         c_all(lambda c: c.wait_send())
 
-    @pl.when(x < 3)
-    def _():
-        each(1, 4, lambda k: w1_copy(k).wait_send())
-        each(1, 16, lambda k: w2_copy(k).wait_send())
-
-    each(0, 3, lambda i: w3_part(i).wait_send())
+    @pl.when(core == 0)
+    def _():
+        each(0, 4, lambda i: w3_copy(i).wait_send())
+
+    @pl.when(sender)
+    def _():
+        w1_copy(1, 0).wait_send()
+        w1_copy(3, 0).wait_send()
+        w1_copy(3, 1).wait_send()
+        for step in range(4):
+            each(1, 16, lambda k, step=step: w2_copy(k, step).wait_send())
 
 
 def shards(tokens, tile_pos, w_qkv, w_out):
@@ -490,10 +521,10 @@
             pltpu.VMEM((HEADS, 16, 128), BF16),
             pltpu.VMEM((ROWS, WIDTH), F32),
             pltpu.VMEM((HEADS, ROWS, 128), F32),
-            pltpu.VMEM((4, 4, 3, 16, WIDTH), BF16),
+            pltpu.VMEM((48, 16, WIDTH), BF16),
             dma((6,)), dma((3,)), dma((3,)), dma((16,)), dma, dma, dma,
             dma((4,)), dma((4,)), dma((16,)), dma((16,)), dma, dma, dma((32,)), dma,
-            dma((4,)), dma((4,)), dma((16,)), dma((12,)), dma((3,)), dma((3,)),
+            dma((5,)), dma((4,)), dma((4, 16)), dma((4,)), dma((4,)), dma((4,)),
             pltpu.SemaphoreType.REGULAR, pltpu.SemaphoreType.REGULAR,
         ],
         compiler_params=pltpu.CompilerParams(

time: 49.9 us -> 48.9 us (0.980)
  the two profiles are of different devices: /device:TPU:1 before, /device:TPU:24 now
where the time goes in v4:
time: 48.9 us; the launch traced here: 48.8 us
  Pallas kernels  47.1 us (96%)
  local copies, waits for them, and re-layouts  1.62 us (3%)
    pallas_call x1, Pallas kernels, shards(): pl.pallas_call(kernel, out_shape=jax.ShapeDtypeStruct((ROWS, WIDTH), BF16...  47.1 us
    unnamed x1, local copies, waits for them, and re-layouts  1.62 us

profile of v4, /device:TPU:24, one launch (start us, length us, event | category | flops | bytes accessed | tf_op | source)
XLA Modules:
  0.0 48.8 jit_solution(1781962540893200912)
XLA Ops:
  0.0 47.1 %dilated_attention.1 = bf16[128,768]{1,0:T(8,128)(2,1)} custom-call(bf16[128,768]{1,0:T(8,128)(2,1)} %tok_hbm.1, s32[2,128]{1,0:T(2,128)} %pos_hbm.1, bf16[768,2304]{1,0:T(8,128)(2,1)} %wqkv_hbm.1, bf16[48,768]{1,0:T(8,128)(2,1)} %wout_hbm.1), custom_call_target="tpu_custom_call" | custom-call | tf_op jit(solution)/shard_map/dilated_attention/pallas_call | solution.py:502
  47.1 1.6 %copy.6 = bf16[128,768]{1,0:T(8,128)(2,1)} copy(bf16[128,768]{1,0:T(8,128)(2,1)} %dilated_attention.1) | data formatting | bytes 393216

commit v5 on v4

--- a/solution.py
+++ b/solution.py
@@ -78,7 +78,7 @@
     att, lse, wall,
     load_sem, emb_send, emb_recv, a_send, a_recv, relay_send, relay_recv,
     kv3_send, kv3_recv, far_send, far_recv, o2_send, o2_recv, c_send, c_recv,
-    w1_send, w1_recv, w2_send, w2_recv, w3_send, w3_recv, past, past_too,
+    w1_send, w1_recv, wx_send, wx_recv, wy_send, wy_recv, wf_send, wf_recv, w3_send, w3_recv, past, past_too,
 ):
     g = lax.axis_index("grp")
     s = lax.axis_index("seq")
@@ -89,7 +89,6 @@
     y = g % 4
     sibling = s + 1 - 2 * core
     across = s + 2 - 4 * (chip % 2)
-    sender = (core == 0) & (x < 3)
 
     def remote(src, dst, send_sem, recv_sem, grp, seq):
         return pltpu.make_async_remote_copy(
@@ -119,14 +118,21 @@
     for item in load_wq:
         item.start()
 
-    my_block = (zh * 4 + y) * 3 + x % 3
+    def part_at(step):
+        return (x - zh - step + 8) % 4
+
+    def block_at(step, off):
+        return (((zh + step) % 4) * 4 + (y + off + 4) % 4) * 3
+
     load_wout = pltpu.make_async_copy(
-        wout_hbm.at[pl.ds(pl.multiple_of(16 * (x % 3), 16), 16)], wall.at[my_block], load_sem.at[5]
+        wout_hbm.at[pl.ds(pl.multiple_of(16 * (part_at(0) % 3), 16), 16)],
+        wall.at[block_at(0, 0) + part_at(0) % 3], load_sem.at[5],
     )
 
-    @pl.when(sender)
-    def _():
-        load_wout.start()
+    def bringing(step, act):
+        pl.when((core == 0) & (part_at(step) < 3))(act)
+
+    bringing(0, load_wout.start)
 
     barrier = pltpu.get_barrier_semaphore()
 
@@ -146,7 +152,9 @@
         greet((g + 12) % 16, s)
         each(0, 16, lambda k: greet(g, 2 * k + 1))
         greet(g, across)
-        each(1, 16, lambda k: greet(zh * 4 + (y + k % 4) % 4, ((x + k // 4) % 4) * 8 + s % 8))
+        each(1, 4, lambda k: greet(g, ((x + k) % 4) * 8 + s % 8))
+        greet(zh * 4 + (y + 1) % 4, s)
+        greet(zh * 4 + (y + 3) % 4, s)
 
     load_tok.wait()
     load_pos.wait()
@@ -201,7 +209,7 @@
 
     @pl.when(core == 0)
     def _():
-        pl.semaphore_wait(barrier, 34)
+        pl.semaphore_wait(barrier, 24)
 
     def a_copy(k):
         h = seat(k)
@@ -237,54 +245,76 @@
         tell(past, (g + 12) % 16)
         each(1, 4, lambda k: tell(past, zh * 4 + (y + k) % 4))
 
-    def block_of(step):
-        return (((zh + step) % 4) * 4 + y) * 3 + x % 3
-
     def w1_copy(k, step):
-        block = wall.at[block_of(step)]
+        block = wall.at[block_at(step, 0) + part_at(step) % 3]
         return remote(
             block, block, w1_send.at[k + step], w1_recv.at[(zh + step) % 4], (g + 4 * k + 16) % 16, s
         )
 
     def w1_wait(step):
-        block = wall.at[block_of(step)]
+        block = wall.at[block_at(step, 0) + part_at(step) % 3]
         pltpu.make_async_copy(block, block, w1_recv.at[(zh + step) % 4]).wait()
 
-    def w2_copy(k, step):
-        block = wall.at[block_of(step)]
+    def wx_copy(step, k):
+        block = wall.at[block_at(step, 0) + part_at(step) % 3]
         return remote(
-            block, block, w2_send.at[step, k], w2_recv.at[(zh + step) % 4],
-            zh * 4 + (y + k % 4) % 4, ((x + k // 4) % 4) * 8 + s % 8,
-        )
-
-    def w2_start(step):
-        each(1, 16, lambda k: w2_copy(k, step).start())
-
-    def w2_wait(step):
-        sem = w2_recv.at[(zh + step) % 4]
-
-        @pl.when(x < 3)
-        def _():
-            pltpu.make_async_copy(wall.at[pl.ds(0, 11)], wall.at[pl.ds(0, 11)], sem).wait()
-
-        @pl.when(x == 3)
-        def _():
-            pltpu.make_async_copy(wall.at[pl.ds(0, 12)], wall.at[pl.ds(0, 12)], sem).wait()
+            block, block, wx_send.at[step, k], wx_recv.at[(zh + step) % 4], g, ((x + k) % 4) * 8 + s % 8
+        )
+
+    def wy_copy(step, way):
+        blocks = wall.at[pl.ds(block_at(step, 0), 3)]
+        return remote(
+            blocks, blocks, wy_send.at[step, way], wy_recv.at[(zh + step) % 4, way],
+            zh * 4 + (y + 1 + 2 * way) % 4, s,
+        )
+
+    def wf_copy(step, way):
+        blocks = wall.at[pl.ds(block_at(step, 2 * way - 1), 3), :, pl.ds(384 * way, 384)]
+        return remote(
+            blocks, blocks, wf_send.at[step, way], wf_recv.at[(zh + step) % 4, way],
+            zh * 4 + (y + 1 + 2 * way) % 4, s,
+        )
 
     def w3_copy(i):
         blocks = wall.at[pl.ds(12 * i, 12)]
         return remote(blocks, blocks, w3_send.at[i], w3_recv.at[i], g, sibling)
 
+    def wx_start(step):
+        def act():
+            each(1, 4, lambda k: wx_copy(step, k).start())
+        bringing(step, act)
+
+    def wy_start(step):
+        sem = wx_recv.at[(zh + step) % 4]
+
+        @pl.when(part_at(step) < 3)
+        def _():
+            pltpu.make_async_copy(wall.at[pl.ds(0, 2)], wall.at[pl.ds(0, 2)], sem).wait()
+
+        @pl.when(part_at(step) == 3)
+        def _():
+            pltpu.make_async_copy(wall.at[pl.ds(0, 3)], wall.at[pl.ds(0, 3)], sem).wait()
+
+        wy_copy(step, 0).start()
+        wy_copy(step, 1).start()
+
+    def wf_start(step):
+        for way in range(2):
+            wy_copy(step, way).wait_recv()
+            wf_copy(step, way).start()
+
     def w3_start(step):
-        w2_wait(step)
+        for way in range(2):
+            wf_copy(step, way).wait_recv()
         w3_copy((zh + step) % 4).start()
 
-    @pl.when(sender)
-    def _():
+    def first_w1():
         load_wout.wait()
         w1_copy(1, 0).start()
         w1_copy(3, 0).start()
-        w2_start(0)
+
+    bringing(0, first_w1)
+    wx_start(0)
 
     def other_rows(slot):
         for j in range(6):
@@ -301,13 +331,24 @@
         pl.semaphore_wait(past, 4)
         each(1, 4, lambda k: tell(past_too, zh * 4 + (y + k) % 4))
 
-    @pl.when(sender)
-    def _():
+    def pass_on():
         w1_wait(1)
         w1_copy(3, 1).start()
-        w1_wait(3)
-        w2_start(1)
-        w2_start(3)
+
+    @pl.when(core == 0)
+    def _():
+        wy_start(0)
+
+    bringing(1, pass_on)
+    wx_start(1)
+    bringing(3, lambda: w1_wait(3))
+    wx_start(3)
+
+    @pl.when(core == 0)
+    def _():
+        wf_start(0)
+        wy_start(1)
+        wy_start(3)
 
     e_own = chip // 8
     relay = remote(recv_a, recv_a, relay_send, relay_recv, g, sibling)
@@ -355,16 +396,26 @@
         lax.fori_loop(0, 4, block, 0)
         give.start()
 
-    @pl.when(sender)
-    def _():
-        w1_wait(2)
-        w2_start(2)
+    bringing(2, lambda: w1_wait(2))
+    wx_start(2)
+
+    @pl.when(core == 0)
+    def _():
+        wf_start(1)
+        wf_start(3)
+        w3_start(0)
 
     send_across.wait_recv()
     send_on.start()
     other_rows(2)
     send_on.wait_recv()
     other_rows(3)
+
+    @pl.when(core == 0)
+    def _():
+        wy_start(2)
+        w3_start(1)
+        w3_start(3)
 
     def first_branch(rho, carry):
         b = (rho + 5) // 8
@@ -387,9 +438,7 @@
 
     @pl.when(core == 0)
     def _():
-        w3_start(0)
-        w3_start(1)
-        w3_start(3)
+        wf_start(2)
 
     def c_copy(k):
         there = 2 * seat(k // 2) + 1 - k % 2
@@ -487,13 +536,19 @@
     def _():
         each(0, 4, lambda i: w3_copy(i).wait_send())
 
-    @pl.when(sender)
-    def _():
+        for step in range(4):
+            for way in range(2):
+                wy_copy(step, way).wait_send()
+                wf_copy(step, way).wait_send()
+
+    def w1_left():
         w1_copy(1, 0).wait_send()
         w1_copy(3, 0).wait_send()
-        w1_copy(3, 1).wait_send()
-        for step in range(4):
-            each(1, 16, lambda k, step=step: w2_copy(k, step).wait_send())
+
+    bringing(0, w1_left)
+    bringing(1, lambda: w1_copy(3, 1).wait_send())
+    for step in range(4):
+        bringing(step, lambda step=step: each(1, 4, lambda k: wx_copy(step, k).wait_send()))
 
 
 def shards(tokens, tile_pos, w_qkv, w_out):
@@ -524,7 +579,7 @@
             pltpu.VMEM((48, 16, WIDTH), BF16),
             dma((6,)), dma((3,)), dma((3,)), dma((16,)), dma, dma, dma,
             dma((4,)), dma((4,)), dma((16,)), dma((16,)), dma, dma, dma((32,)), dma,
-            dma((5,)), dma((4,)), dma((4, 16)), dma((4,)), dma((4,)), dma((4,)),
+            dma((5,)), dma((4,)), dma((4, 4)), dma((4,)), dma((4, 2)), dma((4, 2)), dma((4, 2)), dma((4, 2)), dma((4,)), dma((4,)),
             pltpu.SemaphoreType.REGULAR, pltpu.SemaphoreType.REGULAR,
         ],
         compiler_params=pltpu.CompilerParams(

time: 48.9 us -> 53.1 us (1.086)
  the two profiles are of different devices: /device:TPU:24 before, /device:TPU:1 now
where the time goes in v5:
time: 53.1 us; the launch traced here: 52.9 us
  Pallas kernels  51.3 us (97%)
  local copies, waits for them, and re-layouts  1.62 us (3%)
    pallas_call x1, Pallas kernels, shards(): pl.pallas_call(kernel, out_shape=jax.ShapeDtypeStruct((ROWS, WIDTH), BF16...  51.3 us
    unnamed x1, local copies, waits for them, and re-layouts  1.62 us

profile of v5, /device:TPU:1, one launch (start us, length us, event | category | flops | bytes accessed | tf_op | source)
XLA Modules:
  0.0 52.9 jit_solution(13661094717174613417)
XLA Ops:
  0.0 51.3 %dilated_attention.1 = bf16[128,768]{1,0:T(8,128)(2,1)} custom-call(bf16[128,768]{1,0:T(8,128)(2,1)} %tok_hbm.1, s32[2,128]{1,0:T(2,128)} %pos_hbm.1, bf16[768,2304]{1,0:T(8,128)(2,1)} %wqkv_hbm.1, bf16[48,768]{1,0:T(8,128)(2,1)} %wout_hbm.1), custom_call_target="tpu_custom_call" | custom-call | tf_op jit(solution)/shard_map/dilated_attention/pallas_call | solution.py:557
  51.3 1.6 %copy.6 = bf16[128,768]{1,0:T(8,128)(2,1)} copy(bf16[128,768]{1,0:T(8,128)(2,1)} %dilated_attention.1) | data formatting | bytes 393216

commit v6 on v5

--- a/solution.py
+++ b/solution.py
@@ -76,9 +76,9 @@
     tok_hbm, pos_hbm, wqkv_hbm, wout_hbm, out_ref,
     tok, pos, wq, emb, q_own, kv_all, msg, recv_a, kv3, far, q3, out2, msg_c, recv_c,
     att, lse, wall,
-    load_sem, emb_send, emb_recv, a_send, a_recv, relay_send, relay_recv,
-    kv3_send, kv3_recv, far_send, far_recv, o2_send, o2_recv, c_send, c_recv,
-    w1_send, w1_recv, wx_send, wx_recv, wy_send, wy_recv, wf_send, wf_recv, w3_send, w3_recv, past, past_too,
+    load_sem, emb_send, emb_recv, a_send, a_recv,
+    kv3_send, kv3_recv, far_send, far_recv, c_send, c_recv,
+    w1_send, w1_recv, wx_send, wx_recv, wy_send, wy_recv, wf_send, wf_recv, w3_send, w3_recv, past,
 ):
     g = lax.axis_index("grp")
     s = lax.axis_index("seq")
@@ -234,8 +234,6 @@
     send_across = remote(emb.at[0], emb.at[2], emb_send.at[0], emb_recv.at[0], g, across)
     send_sibling = remote(emb.at[0], emb.at[1], emb_send.at[1], emb_recv.at[1], g, sibling)
     send_on = remote(emb.at[2], emb.at[3], emb_send.at[2], emb_recv.at[2], g, sibling)
-    send_across.start()
-    send_sibling.start()
 
     def tell(sem, grp):
         pl.semaphore_signal(sem, inc=1, device_id=(grp, s), device_id_type=MESH)
@@ -243,7 +241,6 @@
     @pl.when(core == 1)
     def _():
         tell(past, (g + 12) % 16)
-        each(1, 4, lambda k: tell(past, zh * 4 + (y + k) % 4))
 
     def w1_copy(k, step):
         block = wall.at[block_at(step, 0) + part_at(step) % 3]
@@ -315,6 +312,8 @@
 
     bringing(0, first_w1)
     wx_start(0)
+    send_across.start()
+    send_sibling.start()
 
     def other_rows(slot):
         for j in range(6):
@@ -328,8 +327,7 @@
 
     @pl.when(core == 1)
     def _():
-        pl.semaphore_wait(past, 4)
-        each(1, 4, lambda k: tell(past_too, zh * 4 + (y + k) % 4))
+        pl.semaphore_wait(past, 1)
 
     def pass_on():
         w1_wait(1)
@@ -344,15 +342,7 @@
     bringing(3, lambda: w1_wait(3))
     wx_start(3)
 
-    @pl.when(core == 0)
-    def _():
-        wf_start(0)
-        wy_start(1)
-        wy_start(3)
-
     e_own = chip // 8
-    relay = remote(recv_a, recv_a, relay_send, relay_recv, g, sibling)
-    give = remote(out2, out2, o2_send, o2_recv, g, sibling)
 
     def kv3_copy(k):
         block = kv3.at[y]
@@ -360,31 +350,39 @@
 
     def far_copy(k):
         return remote(
-            kv3.at[y, pl.ds(0, 32)], far.at[g], far_send.at[k], far_recv.at[g],
-            ((zh + far_step(k)) % 4) * 4 + (y + 2 + k) % 4, s,
-        )
-
-    def far_step(k):
-        return (k // 4) % 3 + 1
+            kv3.at[y, pl.ds(0, 32)], far.at[4 * y + zh], far_send.at[k], far_recv.at[zh],
+            ((zh + k) % 4) * 4 + y, s,
+        )
+
+    def spread_copy(k):
+        slots = far.at[pl.ds(4 * y, 4)]
+        return remote(slots, slots, far_send.at[k + 4], far_recv.at[4 + y], zh * 4 + (y + k) % 4, s)
 
     @pl.when(core == 1)
     def _():
         pltpu.make_async_copy(recv_a, recv_a, a_recv).wait()
-        relay.start()
         spot = iota((128, 512), 0)
         col = iota((128, 512), 1)
         pick = ((spot % 32) * 16 + 4 * e_own + spot // 32 == col).astype(F32).astype(BF16)
         chosen = dot(pick, recv_a[...].reshape(512, 256)).astype(BF16)
         kv3[y] = chosen[:, 0:128]
         q3[...] = chosen[:, 128:256]
-        pl.semaphore_wait(past_too, 3)
-        each(4, 16, lambda k: far_copy(k).start())
+        far_copy(2).start()
+        far_copy(1).start()
+        far_copy(3).start()
         each(1, 4, lambda k: kv3_copy(k).start())
 
     @pl.when(core == 0)
     def _():
-        relay.wait_recv()
-
+        wf_start(0)
+        wy_start(1)
+        wy_start(3)
+
+    send_across.wait_recv()
+    send_on.start()
+
+    @pl.when(core == 1)
+    def _():
         def block(i, carry):
             rows = pl.ds(pl.multiple_of(128 * i, 128), 128)
             flat = recv_a[...].reshape(512, 256)
@@ -394,7 +392,6 @@
             return carry
 
         lax.fori_loop(0, 4, block, 0)
-        give.start()
 
     bringing(2, lambda: w1_wait(2))
     wx_start(2)
@@ -403,10 +400,7 @@
     def _():
         wf_start(1)
         wf_start(3)
-        w3_start(0)
-
-    send_across.wait_recv()
-    send_on.start()
+
     other_rows(2)
     send_on.wait_recv()
     other_rows(3)
@@ -414,8 +408,7 @@
     @pl.when(core == 0)
     def _():
         wy_start(2)
-        w3_start(1)
-        w3_start(3)
+        w3_start(0)
 
     def first_branch(rho, carry):
         b = (rho + 5) // 8
@@ -434,11 +427,14 @@
             lse[rho + 8 * e] = jnp.broadcast_to(top * SCALE + jnp.log2(total), (ROWS, 128))
         return carry
 
-    lax.fori_loop(0, 4, first_branch, 0)
-
-    @pl.when(core == 0)
-    def _():
+    @pl.when(core == 0)
+    def _():
+        lax.fori_loop(0, 2, first_branch, 0)
         wf_start(2)
+        w3_start(1)
+        w3_start(3)
+        lax.fori_loop(2, 4, first_branch, 0)
+        w3_start(2)
 
     def c_copy(k):
         there = 2 * seat(k // 2) + 1 - k % 2
@@ -452,7 +448,6 @@
     def _():
         each(1, 4, lambda k: pltpu.make_async_copy(kv3.at[0], kv3.at[0], kv3_recv.at[(y + k) % 4]).wait())
         mixed3, level3 = attend(q3[...], kv3[...].reshape(512, 128))
-        give.wait_recv()
 
         def fold(m, a, l):
             rows = pl.ds(4 * e_own + m, 32, stride=16)
@@ -462,10 +457,12 @@
 
         for m in range(4):
             fold(m, mixed3[32 * m : 32 * m + 32], level3[32 * m : 32 * m + 32])
-        for k in range(4):
-            far[zh * 4 + k] = kv3[k, 0:32, :]
-        each(4, 16, lambda k: pltpu.make_async_copy(
-            far.at[0], far.at[0], far_recv.at[((zh + k // 4) % 4) * 4 + k % 4]).wait())
+        far[4 * y + zh] = kv3[y, 0:32, :]
+        each(1, 4, lambda k: pltpu.make_async_copy(far.at[0], far.at[0], far_recv.at[(zh + k) % 4]).wait())
+        each(1, 4, lambda k: spread_copy(k).start())
+        lax.fori_loop(0, 2, first_branch, 0)
+        each(1, 4, lambda k: pltpu.make_async_copy(
+            far.at[pl.ds(0, 4)], far.at[pl.ds(0, 4)], far_recv.at[4 + (y + k) % 4]).wait())
         mixed4, level4 = attend(q3[0:32, :], far[...].reshape(512, 128))
         fold(0, mixed4, level4)
         done = out2[...]
@@ -478,11 +475,7 @@
         c_all(lambda c: c.start())
         pltpu.make_async_copy(msg_c.at[s], recv_c.at[chip], c_recv).start()
 
-    lax.fori_loop(4, 8, first_branch, 0)
-
-    @pl.when(core == 0)
-    def _():
-        w3_start(2)
+    lax.fori_loop(4 - 2 * core, 8, first_branch, 0)
 
     pltpu.make_async_copy(recv_c, recv_c, c_recv).wait()
     for rho in range(8):
@@ -521,15 +514,11 @@
     send_on.wait_send()
     a_all(lambda c: c.wait_send())
 
-    @pl.when(core == 0)
-    def _():
-        give.wait_send()
-
-    @pl.when(core == 1)
-    def _():
-        relay.wait_send()
+    @pl.when(core == 1)
+    def _():
         each(1, 4, lambda k: kv3_copy(k).wait_send())
-        each(4, 16, lambda k: far_copy(k).wait_send())
+        each(1, 4, lambda k: far_copy(k).wait_send())
+        each(1, 4, lambda k: spread_copy(k).wait_send())
         c_all(lambda c: c.wait_send())
 
     @pl.when(core == 0)
@@ -577,10 +566,10 @@
             pltpu.VMEM((ROWS, WIDTH), F32),
             pltpu.VMEM((HEADS, ROWS, 128), F32),
             pltpu.VMEM((48, 16, WIDTH), BF16),
-            dma((6,)), dma((3,)), dma((3,)), dma((16,)), dma, dma, dma,
-            dma((4,)), dma((4,)), dma((16,)), dma((16,)), dma, dma, dma((32,)), dma,
+            dma((6,)), dma((3,)), dma((3,)), dma((16,)), dma,
+            dma((4,)), dma((4,)), dma((8,)), dma((8,)), dma((32,)), dma,
             dma((5,)), dma((4,)), dma((4, 4)), dma((4,)), dma((4, 2)), dma((4, 2)), dma((4, 2)), dma((4, 2)), dma((4,)), dma((4,)),
-            pltpu.SemaphoreType.REGULAR, pltpu.SemaphoreType.REGULAR,
+            pltpu.SemaphoreType.REGULAR,
         ],
         compiler_params=pltpu.CompilerParams(
             collective_id=0, has_side_effects=True, vmem_limit_bytes=60 * 1024 * 1024

time: 53.1 us -> 44.9 us (0.85)
  the two profiles are of different devices: /device:TPU:1 before, /device:TPU:32 now
where the time goes in v6:
time: 44.9 us; the launch traced here: 44.7 us
  Pallas kernels  43.1 us (96%)
  local copies, waits for them, and re-layouts  1.62 us (4%)
    pallas_call x1, Pallas kernels, shards(): pl.pallas_call(kernel, out_shape=jax.ShapeDtypeStruct((ROWS, WIDTH), BF16...  43.1 us
    unnamed x1, local copies, waits for them, and re-layouts  1.62 us

profile of v6, /device:TPU:32, one launch (start us, length us, event | category | flops | bytes accessed | tf_op | source)
XLA Modules:
  0.0 44.7 jit_solution(8419770283029981936)
XLA Ops:
  0.0 43.1 %dilated_attention.1 = bf16[128,768]{1,0:T(8,128)(2,1)} custom-call(bf16[128,768]{1,0:T(8,128)(2,1)} %tok_hbm.1, s32[2,128]{1,0:T(2,128)} %pos_hbm.1, bf16[768,2304]{1,0:T(8,128)(2,1)} %wqkv_hbm.1, bf16[48,768]{1,0:T(8,128)(2,1)} %wout_hbm.1), custom_call_target="tpu_custom_call" | custom-call | tf_op jit(solution)/shard_map/dilated_attention/pallas_call | solution.py:546
  43.1 1.6 %copy.6 = bf16[128,768]{1,0:T(8,128)(2,1)} copy(bf16[128,768]{1,0:T(8,128)(2,1)} %dilated_attention.1) | data formatting | bytes 393216

commit v7 on v6

--- a/solution.py
+++ b/solution.py
@@ -170,6 +170,81 @@
         turn = ((lane % 384) >= 192).astype(jnp.int32)
         value = sine(spot * omega(lane), turn)
         emb[0, :, cols] = (dot(order_bf, tok[:, cols]) + value).astype(BF16)
+
+    def w1_copy(k, step):
+        block = wall.at[block_at(step, 0) + part_at(step) % 3]
+        return remote(
+            block, block, w1_send.at[k + step], w1_recv.at[(zh + step) % 4], (g + 4 * k + 16) % 16, s
+        )
+
+    def w1_wait(step):
+        block = wall.at[block_at(step, 0) + part_at(step) % 3]
+        pltpu.make_async_copy(block, block, w1_recv.at[(zh + step) % 4]).wait()
+
+    def wx_copy(step, k):
+        block = wall.at[block_at(step, 0) + part_at(step) % 3]
+        return remote(
+            block, block, wx_send.at[step, k], wx_recv.at[(zh + step) % 4], g, ((x + k) % 4) * 8 + s % 8
+        )
+
+    def wy_copy(step, way):
+        blocks = wall.at[pl.ds(block_at(step, 0), 3)]
+        return remote(
+            blocks, blocks, wy_send.at[step, way], wy_recv.at[(zh + step) % 4, way],
+            zh * 4 + (y + 1 + 2 * way) % 4, s,
+        )
+
+    def wf_copy(step, way):
+        blocks = wall.at[pl.ds(block_at(step, 2 * way - 1), 3), :, pl.ds(384 * way, 384)]
+        return remote(
+            blocks, blocks, wf_send.at[step, way], wf_recv.at[(zh + step) % 4, way],
+            zh * 4 + (y + 1 + 2 * way) % 4, s,
+        )
+
+    def w3_copy(i):
+        blocks = wall.at[pl.ds(12 * i, 12)]
+        return remote(blocks, blocks, w3_send.at[i], w3_recv.at[i], g, sibling)
+
+    def wx_start(step):
+        def act():
+            each(1, 4, lambda k: wx_copy(step, k).start())
+        bringing(step, act)
+
+    def wy_start(step):
+        sem = wx_recv.at[(zh + step) % 4]
+
+        @pl.when(part_at(step) < 3)
+        def _():
+            pltpu.make_async_copy(wall.at[pl.ds(0, 2)], wall.at[pl.ds(0, 2)], sem).wait()
+
+        @pl.when(part_at(step) == 3)
+        def _():
+            pltpu.make_async_copy(wall.at[pl.ds(0, 3)], wall.at[pl.ds(0, 3)], sem).wait()
+
+        wy_copy(step, 0).start()
+        wy_copy(step, 1).start()
+
+    def wf_start(step):
+        for way in range(2):
+            wy_copy(step, way).wait_recv()
+            wf_copy(step, way).start()
+
+    def w3_start(step):
+        for way in range(2):
+            wf_copy(step, way).wait_recv()
+        w3_copy((zh + step) % 4).start()
+
+    def first_w1():
+        load_wout.wait()
+        w1_copy(1, 0).start()
+        w1_copy(3, 0).start()
+
+    @pl.when(core == 0)
+    def _():
+        pl.semaphore_wait(barrier, 24)
+
+    bringing(0, first_w1)
+    wx_start(0)
 
     for i in range(3):
         load_wq[i].wait()
@@ -207,10 +282,6 @@
     def _():
         pl.semaphore_wait(barrier, 36)
 
-    @pl.when(core == 0)
-    def _():
-        pl.semaphore_wait(barrier, 24)
-
     def a_copy(k):
         h = seat(k)
         return remote(msg.at[h], recv_a.at[s], a_send.at[k], a_recv, g, 2 * h + 1)
@@ -242,76 +313,6 @@
     def _():
         tell(past, (g + 12) % 16)
 
-    def w1_copy(k, step):
-        block = wall.at[block_at(step, 0) + part_at(step) % 3]
-        return remote(
-            block, block, w1_send.at[k + step], w1_recv.at[(zh + step) % 4], (g + 4 * k + 16) % 16, s
-        )
-
-    def w1_wait(step):
-        block = wall.at[block_at(step, 0) + part_at(step) % 3]
-        pltpu.make_async_copy(block, block, w1_recv.at[(zh + step) % 4]).wait()
-
-    def wx_copy(step, k):
-        block = wall.at[block_at(step, 0) + part_at(step) % 3]
-        return remote(
-            block, block, wx_send.at[step, k], wx_recv.at[(zh + step) % 4], g, ((x + k) % 4) * 8 + s % 8
-        )
-
-    def wy_copy(step, way):
-        blocks = wall.at[pl.ds(block_at(step, 0), 3)]
-        return remote(
-            blocks, blocks, wy_send.at[step, way], wy_recv.at[(zh + step) % 4, way],
-            zh * 4 + (y + 1 + 2 * way) % 4, s,
-        )
-
-    def wf_copy(step, way):
-        blocks = wall.at[pl.ds(block_at(step, 2 * way - 1), 3), :, pl.ds(384 * way, 384)]
-        return remote(
-            blocks, blocks, wf_send.at[step, way], wf_recv.at[(zh + step) % 4, way],
-            zh * 4 + (y + 1 + 2 * way) % 4, s,
-        )
-
-    def w3_copy(i):
-        blocks = wall.at[pl.ds(12 * i, 12)]
-        return remote(blocks, blocks, w3_send.at[i], w3_recv.at[i], g, sibling)
-
-    def wx_start(step):
-        def act():
-            each(1, 4, lambda k: wx_copy(step, k).start())
-        bringing(step, act)
-
-    def wy_start(step):
-        sem = wx_recv.at[(zh + step) % 4]
-
-        @pl.when(part_at(step) < 3)
-        def _():
-            pltpu.make_async_copy(wall.at[pl.ds(0, 2)], wall.at[pl.ds(0, 2)], sem).wait()
-
-        @pl.when(part_at(step) == 3)
-        def _():
-            pltpu.make_async_copy(wall.at[pl.ds(0, 3)], wall.at[pl.ds(0, 3)], sem).wait()
-
-        wy_copy(step, 0).start()
-        wy_copy(step, 1).start()
-
-    def wf_start(step):
-        for way in range(2):
-            wy_copy(step, way).wait_recv()
-            wf_copy(step, way).start()
-
-    def w3_start(step):
-        for way in range(2):
-            wf_copy(step, way).wait_recv()
-        w3_copy((zh + step) % 4).start()
-
-    def first_w1():
-        load_wout.wait()
-        w1_copy(1, 0).start()
-        w1_copy(3, 0).start()
-
-    bringing(0, first_w1)
-    wx_start(0)
     send_across.start()
     send_sibling.start()
 
@@ -410,7 +411,12 @@
         wy_start(2)
         w3_start(0)
 
-    def first_branch(rho, carry):
+    def first_branch(pair, carry):
+        heads_of(2 * pair)
+        heads_of(2 * pair + 1)
+        return carry
+
+    def heads_of(rho):
         b = (rho + 5) // 8
         off = 48 * rho - 128 * b
         lane = iota((1, 256), 1)
@@ -425,15 +431,14 @@
             mixed = dot(weights.astype(BF16), kv_all[:, win_v]) * (1.0 / total)
             att[:, win] = jnp.where(mine, mixed, att[:, win])
             lse[rho + 8 * e] = jnp.broadcast_to(top * SCALE + jnp.log2(total), (ROWS, 128))
-        return carry
-
-    @pl.when(core == 0)
-    def _():
-        lax.fori_loop(0, 2, first_branch, 0)
+
+    @pl.when(core == 0)
+    def _():
+        lax.fori_loop(0, 1, first_branch, 0)
         wf_start(2)
         w3_start(1)
         w3_start(3)
-        lax.fori_loop(2, 4, first_branch, 0)
+        lax.fori_loop(1, 2, first_branch, 0)
         w3_start(2)
 
     def c_copy(k):
@@ -458,9 +463,10 @@
         for m in range(4):
             fold(m, mixed3[32 * m : 32 * m + 32], level3[32 * m : 32 * m + 32])
         far[4 * y + zh] = kv3[y, 0:32, :]
+        lax.fori_loop(0, 1, first_branch, 0)
         each(1, 4, lambda k: pltpu.make_async_copy(far.at[0], far.at[0], far_recv.at[(zh + k) % 4]).wait())
         each(1, 4, lambda k: spread_copy(k).start())
-        lax.fori_loop(0, 2, first_branch, 0)
+        lax.fori_loop(1, 2, first_branch, 0)
         each(1, 4, lambda k: pltpu.make_async_copy(
             far.at[pl.ds(0, 4)], far.at[pl.ds(0, 4)], far_recv.at[4 + (y + k) % 4]).wait())
         mixed4, level4 = attend(q3[0:32, :], far[...].reshape(512, 128))
@@ -475,7 +481,7 @@
         c_all(lambda c: c.start())
         pltpu.make_async_copy(msg_c.at[s], recv_c.at[chip], c_recv).start()
 
-    lax.fori_loop(4 - 2 * core, 8, first_branch, 0)
+    lax.fori_loop(2, 4, first_branch, 0)
 
     pltpu.make_async_copy(recv_c, recv_c, c_recv).wait()
     for rho in range(8):

time: 44.9 us -> 43.6 us (0.971)
  the two profiles are of different devices: /device:TPU:32 before, /device:TPU:1 now
where the time goes in v7:
time: 43.6 us; the launch traced here: 43.5 us
  Pallas kernels  41.8 us (96%)
  local copies, waits for them, and re-layouts  1.62 us (4%)
    pallas_call x1, Pallas kernels, shards(): pl.pallas_call(kernel, out_shape=jax.ShapeDtypeStruct((ROWS, WIDTH), BF16...  41.8 us
    unnamed x1, local copies, waits for them, and re-layouts  1.62 us

profile of v7, /device:TPU:1, one launch (start us, length us, event | category | flops | bytes accessed | tf_op | source)
XLA Modules:
  0.0 43.5 jit_solution(15051639837917961779)
XLA Ops:
  0.0 41.8 %dilated_attention.1 = bf16[128,768]{1,0:T(8,128)(2,1)} custom-call(bf16[128,768]{1,0:T(8,128)(2,1)} %tok_hbm.1, s32[2,128]{1,0:T(2,128)} %pos_hbm.1, bf16[768,2304]{1,0:T(8,128)(2,1)} %wqkv_hbm.1, bf16[48,768]{1,0:T(8,128)(2,1)} %wout_hbm.1), custom_call_target="tpu_custom_call" | custom-call | tf_op jit(solution)/shard_map/dilated_attention/pallas_call | solution.py:552
  41.9 1.6 %copy.6 = bf16[128,768]{1,0:T(8,128)(2,1)} copy(bf16[128,768]{1,0:T(8,128)(2,1)} %dilated_attention.1) | data formatting | bytes 393216

commit v8 on v7

--- a/solution.py
+++ b/solution.py
@@ -434,12 +434,12 @@
 
     @pl.when(core == 0)
     def _():
-        lax.fori_loop(0, 1, first_branch, 0)
         wf_start(2)
         w3_start(1)
         w3_start(3)
+        lax.fori_loop(0, 1, first_branch, 0)
+        w3_start(2)
         lax.fori_loop(1, 2, first_branch, 0)
-        w3_start(2)
 
     def c_copy(k):
         there = 2 * seat(k // 2) + 1 - k % 2

time: 43.6 us -> 45 us (1.032)
  the two profiles are of different devices: /device:TPU:1 before, /device:TPU:32 now
where the time goes in v8:
time: 45 us; the launch traced here: 44.9 us
  Pallas kernels  43.2 us (96%)
  local copies, waits for them, and re-layouts  1.62 us (4%)
    pallas_call x1, Pallas kernels, shards(): pl.pallas_call(kernel, out_shape=jax.ShapeDtypeStruct((ROWS, WIDTH), BF16...  43.2 us
    unnamed x1, local copies, waits for them, and re-layouts  1.62 us

profile of v8, /device:TPU:32, one launch (start us, length us, event | category | flops | bytes accessed | tf_op | source)
XLA Modules:
  0.0 44.9 jit_solution(1546912905752339339)
XLA Ops:
  0.0 43.2 %dilated_attention.1 = bf16[128,768]{1,0:T(8,128)(2,1)} custom-call(bf16[128,768]{1,0:T(8,128)(2,1)} %tok_hbm.1, s32[2,128]{1,0:T(2,128)} %pos_hbm.1, bf16[768,2304]{1,0:T(8,128)(2,1)} %wqkv_hbm.1, bf16[48,768]{1,0:T(8,128)(2,1)} %wout_hbm.1), custom_call_target="tpu_custom_call" | custom-call | tf_op jit(solution)/shard_map/dilated_attention/pallas_call | solution.py:552
  43.2 1.6 %copy.6 = bf16[128,768]{1,0:T(8,128)(2,1)} copy(bf16[128,768]{1,0:T(8,128)(2,1)} %dilated_attention.1) | data formatting | bytes 393216
